TPU v7x, 32 devices: a whole 2x2x4 slice. The times are simulated.
32 devices in a mesh: rows: 8 (over z, core), pos: 4 (over y, x).
Axes of the slice: x: 2, y: 2, z: 4, core: 2. Of those that a mesh axis runs over, the one named last changes fastest.
Arguments:
- activations: bfloat16 [8, 2048, 1024], P('rows', 'pos'), may hold values from -6 to 6
- out_grad: bfloat16 [8, 2048, 1024], P('rows', 'pos'), may hold values from -6 to 6
- doc_bounds: int32 [8, 3], P('rows'), may hold values from 0 to 2048, as said below
- doc_ids: int32 [8, 2048], P('rows'), may hold values from 0 to 2, as said below
- pre_gain: bfloat16 [1024], P(('rows', 'pos')), may hold values from 0.5 to 1.5
- pre_bias: bfloat16 [1024], P(('rows', 'pos')), may hold values from -1.25 to 1.25
- in_weight: bfloat16 [1024, 3, 1024], P(('rows', 'pos')), may hold values from -0.1875 to 0.1875
- in_bias: bfloat16 [3, 1024], P(None, ('rows', 'pos')), may hold values from -1.25 to 1.25
- short_weight: bfloat16 [3, 3, 1024], P(None, None, ('rows', 'pos')), may hold values from -3.5 to 3.5
- short_bias: bfloat16 [3, 1024], P(None, ('rows', 'pos')), may hold values from -1.25 to 1.25
- skip_gain: bfloat16 [1024], P(('rows', 'pos')), may hold values from -6 to 6
- out_weight: bfloat16 [1024, 1024], P(('rows', 'pos')), may hold values from -0.1875 to 0.1875
- out_bias: bfloat16 [1024], P(('rows', 'pos')), may hold values from -1.25 to 1.25
- post_gain: bfloat16 [1024], P(('rows', 'pos')), may hold values from 0.5 to 1.5
- post_bias: bfloat16 [1024], P(('rows', 'pos')), may hold values from -1.25 to 1.25
- up_weight: bfloat16 [1024, 4096], P(('rows', 'pos')), may hold values from -0.1875 to 0.1875
- up_bias: bfloat16 [4096], P(('rows', 'pos')), may hold values from -1.25 to 1.25
- down_weight: bfloat16 [4096, 1024], P(('rows', 'pos')), may hold values from -0.09375 to 0.09375
- down_bias: bfloat16 [1024], P(('rows', 'pos')), may hold values from -1.25 to 1.25
- filter_one: bfloat16 [33, 64], replicated, may hold values from -1 to 1
- filter_bias_one: bfloat16 [64], replicated, may hold values from -3 to 3
- filter_two: bfloat16 [64, 64], replicated, may hold values from -0.75 to 0.75
- filter_bias_two: bfloat16 [64], replicated, may hold values from -3 to 3
- filter_freq: bfloat16 [64], replicated, may hold values from 0.5 to 3
- filter_three: bfloat16 [64, 1024], P(None, ('rows', 'pos')), may hold values from -0.078125 to 0.078125
Outputs:
- result: bfloat16 [8, 2048, 1024], P('rows', 'pos')
- input_grad: bfloat16 [8, 2048, 1024], P('rows', 'pos')
- pre_gain_grad: float32 [1024], P(('rows', 'pos'))
- pre_bias_grad: float32 [1024], P(('rows', 'pos'))
- in_weight_grad: float32 [1024, 3, 1024], P(('rows', 'pos'))
- in_bias_grad: float32 [3, 1024], P(None, ('rows', 'pos'))
- short_weight_grad: float32 [3, 3, 1024], P(None, None, ('rows', 'pos'))
- short_bias_grad: float32 [3, 1024], P(None, ('rows', 'pos'))
- skip_gain_grad: float32 [1024], P(('rows', 'pos'))
- out_weight_grad: float32 [1024, 1024], P(('rows', 'pos'))
- out_bias_grad: float32 [1024], P(('rows', 'pos'))
- post_gain_grad: float32 [1024], P(('rows', 'pos'))
- post_bias_grad: float32 [1024], P(('rows', 'pos'))
- up_weight_grad: float32 [1024, 4096], P(('rows', 'pos'))
- up_bias_grad: float32 [4096], P(('rows', 'pos'))
- down_weight_grad: float32 [4096, 1024], P(('rows', 'pos'))
- down_bias_grad: float32 [1024], P(('rows', 'pos'))
- filter_one_grad: float32 [33, 64], replicated
- filter_bias_one_grad: float32 [64], replicated
- filter_two_grad: float32 [64, 64], replicated
- filter_bias_two_grad: float32 [64], replicated
- filter_freq_grad: float32 [64], replicated
- filter_three_grad: float32 [64, 1024], P(None, ('rows', 'pos'))
Inputs may be any that keep to these rules, and one draw needn't show every extreme that they name: doc_bounds[r, 0] is 0 and the later entries of row r are the first tokens of its second, third and later documents, rising; a row holds 1 to 3 documents and the slots after its last document hold 2048; some row holds 3 documents and some row a single one. doc_ids[r, t] is the number of entries of doc_bounds[r, 1:] that are at most t.
All inputs are finite; a program needn't handle non-finite values.
Results may differ from a plain program's by a relative error of at most 0.011.
Values may be sent and summed in bfloat16 or wider, within the bound.
A program may use at most 320 MiB of HBM per device.

v0:
```python
import math

import jax
import jax.numpy as jnp
from jax import lax
from jax.sharding import PartitionSpec as P

HIGHEST = lax.Precision.HIGHEST
TRANSFORM_PRECISION = lax.Precision.HIGH


def layer_norm(values, norm_gain, norm_shift):
    centre = values - jnp.mean(values, axis=-1, keepdims=True)
    spread = jnp.mean(centre * centre, axis=-1, keepdims=True)
    return centre * lax.rsqrt(spread + 1e-05) * norm_gain + norm_shift


def gelu_tanh(values):
    return jax.nn.gelu(values, approximate=True)


def filter_net(
    places, channels, length, model_width, w_one, b_one, w_two, b_two, frequency, w_three
):
    scaled = places / (length - 1)
    band_count = (w_one.shape[0] - 1) // 2
    ladder = 0.0001 + (band_count - 1 - 0.0001) * jnp.arange(band_count).astype(places.dtype) / (
        band_count - 1
    )
    angles = 2.0 * math.pi / length * places[:, None] * ladder[None, :]
    embedding = jnp.concatenate([scaled[:, None], jnp.cos(angles), -jnp.sin(angles)], axis=1)
    layer_one = jnp.sin(frequency * (jnp.dot(embedding, w_one, precision=HIGHEST) + b_one))
    layer_two = jnp.sin(frequency * (jnp.dot(layer_one, w_two, precision=HIGHEST) + b_two))
    kernel = jnp.dot(layer_two, w_three, precision=HIGHEST)
    slow_rate = math.log(0.01) / 1.5
    fast_rate = math.log(0.01) / 0.3
    decay_rates = jnp.abs(slow_rate + (fast_rate - slow_rate) * channels / (model_width - 1))
    return kernel * (jnp.exp(-scaled[:, None] * decay_rates[None, :]) + 0.05)


def doc_offsets(bounds, length):
    places = jnp.arange(length, dtype=jnp.int32)
    starts = jnp.max(
        jnp.where(bounds[:, None, :] <= places[None, :, None], bounds[:, None, :], 0), axis=2
    )
    return places[None, :] - starts


def short_conv(mixed, tap_weight, tap_bias, offsets):
    length = mixed.shape[1]
    total = jnp.zeros_like(mixed) + tap_bias
    for tap_index in range(tap_weight.shape[0]):
        moved = jnp.pad(mixed, ((0, 0), (tap_index, 0), (0, 0), (0, 0)))[:, :length]
        usable = (offsets >= tap_index)[:, :, None, None]
        total = total + tap_weight[tap_index] * jnp.where(usable, moved, 0.0)
    return total


def dft_tables(total_len):
    outer_len = 2 ** ((total_len.bit_length() - 1) // 2)
    inner_len = total_len // outer_len
    outer_idx = jnp.arange(outer_len, dtype=jnp.int32)
    inner_idx = jnp.arange(inner_len, dtype=jnp.int32)
    first_turn = outer_idx[:, None] * outer_idx[None, : outer_len // 2] % outer_len
    first_angle = 2.0 * math.pi / outer_len * first_turn.astype(jnp.float32)
    twist_turn = outer_idx[:, None] * inner_idx[None, :] % total_len
    twist_angle = 2.0 * math.pi / total_len * twist_turn.astype(jnp.float32)
    last_turn = inner_idx[:, None] * inner_idx[None, :] % inner_len
    last_angle = 2.0 * math.pi / inner_len * last_turn.astype(jnp.float32)
    return (
        jnp.cos(first_angle),
        jnp.sin(first_angle),
        jnp.cos(twist_angle)[None, :, :, None],
        jnp.sin(twist_angle)[None, :, :, None],
        jnp.cos(last_angle),
        jnp.sin(last_angle),
        outer_len,
        inner_len,
    )


def spectrum(signal, tables):
    first_cos, first_sin, twist_cos, twist_sin, last_cos, last_sin, outer_len, inner_len = tables
    blocks = signal.reshape(signal.shape[0], outer_len // 2, inner_len, signal.shape[2])
    section_re = jnp.einsum("kn,bnmc->bkmc", first_cos, blocks, precision=TRANSFORM_PRECISION)
    section_im = -jnp.einsum("kn,bnmc->bkmc", first_sin, blocks, precision=TRANSFORM_PRECISION)
    turned_re = section_re * twist_cos + section_im * twist_sin
    turned_im = section_im * twist_cos - section_re * twist_sin
    spec_re = jnp.einsum(
        "qm,bkmc->bkqc", last_cos, turned_re, precision=TRANSFORM_PRECISION
    ) + jnp.einsum("qm,bkmc->bkqc", last_sin, turned_im, precision=TRANSFORM_PRECISION)
    spec_im = jnp.einsum(
        "qm,bkmc->bkqc", last_cos, turned_im, precision=TRANSFORM_PRECISION
    ) - jnp.einsum("qm,bkmc->bkqc", last_sin, turned_re, precision=TRANSFORM_PRECISION)
    return (spec_re, spec_im)


def inverse(spec_pair, tables):
    first_cos, first_sin, twist_cos, twist_sin, last_cos, last_sin, outer_len, inner_len = tables
    spec_re, spec_im = spec_pair
    back_re = jnp.einsum(
        "qm,bkqc->bkmc", last_cos, spec_re, precision=TRANSFORM_PRECISION
    ) - jnp.einsum("qm,bkqc->bkmc", last_sin, spec_im, precision=TRANSFORM_PRECISION)
    back_im = jnp.einsum(
        "qm,bkqc->bkmc", last_cos, spec_im, precision=TRANSFORM_PRECISION
    ) + jnp.einsum("qm,bkqc->bkmc", last_sin, spec_re, precision=TRANSFORM_PRECISION)
    turned_re = back_re * twist_cos - back_im * twist_sin
    turned_im = back_im * twist_cos + back_re * twist_sin
    signal = jnp.einsum(
        "kn,bkmc->bnmc", first_cos, turned_re, precision=TRANSFORM_PRECISION
    ) - jnp.einsum("kn,bkmc->bnmc", first_sin, turned_im, precision=TRANSFORM_PRECISION)
    batch_rows = signal.shape[0]
    channel_count = signal.shape[3]
    return signal.reshape(batch_rows, outer_len // 2 * inner_len, channel_count) / (
        outer_len * inner_len
    )


def long_conv(signal, filt_spec, doc_rows, slot_count, tables):
    total = jnp.zeros_like(signal)
    for doc_slot in range(slot_count):
        inside = (doc_rows == doc_slot)[:, :, None]
        masked = jnp.where(inside, signal, 0.0)
        spec_re, spec_im = spectrum(masked, tables)
        filt_re, filt_im = filt_spec
        piece = inverse(
            (spec_re * filt_re - spec_im * filt_im, spec_re * filt_im + spec_im * filt_re), tables
        )
        total = total + jnp.where(inside, piece, 0.0)
    return total


def mixer(mixed, tap_weight, tap_bias, skip_part, filt, offsets, doc_rows, slot_count, tables):
    conv = short_conv(mixed, tap_weight, tap_bias, offsets)
    post_gate = conv[:, :, 0]
    pre_gate = conv[:, :, 1]
    values = conv[:, :, 2]
    gated = values * pre_gate
    filt_spec = spectrum(filt[None], tables)
    mixed_out = long_conv(gated, filt_spec, doc_rows, slot_count, tables) + skip_part * gated
    return post_gate * mixed_out


def widen(part_grad, start, model_width, axis_num):
    shape_full = part_grad.shape[:axis_num] + (model_width,) + part_grad.shape[axis_num + 1 :]
    return lax.dynamic_update_slice_in_dim(
        jnp.zeros(shape_full, jnp.float32), part_grad, start, axis_num
    )


def on_device(
    activations,
    out_grad,
    doc_bounds,
    doc_ids,
    pre_gain,
    pre_bias,
    in_weight,
    in_bias,
    short_weight,
    short_bias,
    skip_gain,
    out_weight,
    out_bias,
    post_gain,
    post_bias,
    up_weight,
    up_bias,
    down_weight,
    down_bias,
    filter_one,
    filter_bias_one,
    filter_two,
    filter_bias_two,
    filter_freq,
    filter_three,
):
    single = jnp.float32
    half = jnp.bfloat16
    (
        pre_gain_all,
        pre_bias_all,
        in_weight_all,
        in_bias_all,
        short_weight_all,
        short_bias_all,
        skip_all,
        out_weight_all,
        out_bias_all,
        post_gain_all,
        post_bias_all,
        up_weight_all,
        up_bias_all,
        down_weight_all,
        down_bias_all,
        filter_three_all,
    ) = (
        lax.all_gather(pre_gain, ("rows", "pos"), axis=0, tiled=True),
        lax.all_gather(pre_bias, ("rows", "pos"), axis=0, tiled=True),
        lax.all_gather(in_weight, ("rows", "pos"), axis=0, tiled=True),
        lax.all_gather(in_bias, ("rows", "pos"), axis=1, tiled=True),
        lax.all_gather(short_weight, ("rows", "pos"), axis=2, tiled=True),
        lax.all_gather(short_bias, ("rows", "pos"), axis=1, tiled=True),
        lax.all_gather(skip_gain, ("rows", "pos"), axis=0, tiled=True),
        lax.all_gather(out_weight, ("rows", "pos"), axis=0, tiled=True),
        lax.all_gather(out_bias, ("rows", "pos"), axis=0, tiled=True),
        lax.all_gather(post_gain, ("rows", "pos"), axis=0, tiled=True),
        lax.all_gather(post_bias, ("rows", "pos"), axis=0, tiled=True),
        lax.all_gather(up_weight, ("rows", "pos"), axis=0, tiled=True),
        lax.all_gather(up_bias, ("rows", "pos"), axis=0, tiled=True),
        lax.all_gather(down_weight, ("rows", "pos"), axis=0, tiled=True),
        lax.all_gather(down_bias, ("rows", "pos"), axis=0, tiled=True),
        lax.all_gather(filter_three, ("rows", "pos"), axis=1, tiled=True),
    )
    pos_count = lax.axis_size("pos")
    pos_index = lax.axis_index("pos")
    model_width = activations.shape[2]
    part_len = activations.shape[1]
    full_len = part_len * pos_count
    chan_width = model_width // pos_count
    chan_start = pos_index * chan_width
    slot_count = doc_bounds.shape[1]
    tables = dft_tables(2 * full_len)
    offsets = doc_offsets(doc_bounds, full_len)
    inner_params = (
        filter_one.astype(single),
        filter_bias_one.astype(single),
        filter_two.astype(single),
        filter_bias_two.astype(single),
        filter_freq.astype(single),
    )
    places = (pos_index * part_len + jnp.arange(part_len, dtype=jnp.int32)).astype(single)
    channels = jnp.arange(model_width, dtype=jnp.int32).astype(single)

    def filter_rows(w_one, b_one, w_two, b_two, frequency, w_three):
        return filter_net(
            places, channels, full_len, model_width, w_one, b_one, w_two, b_two, frequency, w_three
        )

    filter_part, filter_back = jax.vjp(filter_rows, *inner_params, filter_three_all.astype(single))
    filt = lax.all_to_all(filter_part, "pos", split_axis=1, concat_axis=0, tiled=True)
    inputs_f = activations.astype(single)
    normed, pre_back = jax.vjp(
        layer_norm, inputs_f, pre_gain_all.astype(single), pre_bias_all.astype(single)
    )
    normed_q = normed.astype(half)
    projected = jnp.einsum(
        "rtd,dke->rtke", normed_q, in_weight_all, preferred_element_type=single
    ) + in_bias_all.astype(single)
    mixed_in = lax.all_to_all(
        projected.astype(half), "pos", split_axis=3, concat_axis=1, tiled=True
    )
    tap_weight = lax.dynamic_slice_in_dim(
        short_weight_all.astype(single), chan_start, chan_width, 2
    )
    tap_bias = lax.dynamic_slice_in_dim(short_bias_all.astype(single), chan_start, chan_width, 1)
    skip_part = lax.dynamic_slice_in_dim(skip_all.astype(single), chan_start, chan_width, 0)

    def mixer_local(mixed_f, tap_w, tap_b, skip_p, filt_p):
        return mixer(mixed_f, tap_w, tap_b, skip_p, filt_p, offsets, doc_ids, slot_count, tables)

    branch, mixer_back = jax.vjp(
        mixer_local, mixed_in.astype(single), tap_weight, tap_bias, skip_part, filt
    )
    branch_tokens = lax.all_to_all(
        branch.astype(half), "pos", split_axis=1, concat_axis=2, tiled=True
    )
    residual = (
        inputs_f
        + jnp.einsum("rtc,cd->rtd", branch_tokens, out_weight_all, preferred_element_type=single)
        + out_bias_all.astype(single)
    )
    normed_two, post_back = jax.vjp(
        layer_norm, residual, post_gain_all.astype(single), post_bias_all.astype(single)
    )
    normed_two_q = normed_two.astype(half)
    hidden_pre = jnp.einsum(
        "rtd,df->rtf", normed_two_q, up_weight_all, preferred_element_type=single
    ) + up_bias_all.astype(single)
    hidden, gelu_back = jax.vjp(gelu_tanh, hidden_pre)
    hidden_q = hidden.astype(half)
    result = (
        residual
        + jnp.einsum("rtf,fd->rtd", hidden_q, down_weight_all, preferred_element_type=single)
        + down_bias_all.astype(single)
    )
    grad_out_f = out_grad.astype(single)
    down_grad = jnp.einsum("rtf,rtd->fd", hidden_q, out_grad, preferred_element_type=single)
    down_bias_grad = jnp.sum(grad_out_f, axis=(0, 1))
    grad_hidden = jnp.einsum(
        "rtd,fd->rtf", out_grad, down_weight_all, preferred_element_type=single
    )
    grad_pre = gelu_back(grad_hidden)[0]
    up_bias_grad = jnp.sum(grad_pre, axis=(0, 1))
    grad_pre_q = grad_pre.astype(half)
    up_grad = jnp.einsum("rtd,rtf->df", normed_two_q, grad_pre_q, preferred_element_type=single)
    grad_normed_two = jnp.einsum(
        "rtf,df->rtd", grad_pre_q, up_weight_all, preferred_element_type=single
    )
    grad_res_part, post_gain_grad, post_bias_grad = post_back(grad_normed_two)
    grad_residual = grad_out_f + grad_res_part
    out_bias_grad = jnp.sum(grad_residual, axis=(0, 1))
    grad_res_q = grad_residual.astype(half)
    out_grad_w = jnp.einsum("rtc,rtd->cd", branch_tokens, grad_res_q, preferred_element_type=single)
    branch_grad = jnp.einsum(
        "rtd,cd->rtc", grad_res_q, out_weight_all, preferred_element_type=single
    )
    branch_grad_ch = lax.all_to_all(
        branch_grad.astype(half), "pos", split_axis=2, concat_axis=1, tiled=True
    )
    grad_mixed_in, tap_w_grad, tap_b_grad, skip_p_grad, filt_grad = mixer_back(
        branch_grad_ch.astype(single)
    )
    grad_tokens = lax.all_to_all(
        grad_mixed_in.astype(half), "pos", split_axis=1, concat_axis=3, tiled=True
    )
    in_bias_grad = jnp.sum(grad_tokens.astype(single), axis=(0, 1))
    in_grad_w = jnp.einsum("rtd,rtke->dke", normed_q, grad_tokens, preferred_element_type=single)
    grad_normed = jnp.einsum(
        "rtke,dke->rtd", grad_tokens, in_weight_all, preferred_element_type=single
    )
    grad_input_part, pre_gain_grad, pre_bias_grad = pre_back(grad_normed)
    input_grad = (grad_residual + grad_input_part).astype(half)
    filt_grad_rows = lax.all_to_all(
        filt_grad.astype(jnp.bfloat16), "pos", split_axis=0, concat_axis=1, tiled=True
    ).astype(filt_grad.dtype)
    inner_grads = filter_back(filt_grad_rows)
    three_grad = inner_grads[5]
    short_w_grad = widen(tap_w_grad, chan_start, model_width, 2)
    short_b_grad = widen(tap_b_grad, chan_start, model_width, 1)
    skip_grad = widen(skip_p_grad, chan_start, model_width, 0)
    summed = (
        lax.psum_scatter(pre_gain_grad, ("rows", "pos"), scatter_dimension=0, tiled=True),
        lax.psum_scatter(pre_bias_grad, ("rows", "pos"), scatter_dimension=0, tiled=True),
        lax.psum_scatter(in_grad_w, ("rows", "pos"), scatter_dimension=0, tiled=True),
        lax.psum_scatter(in_bias_grad, ("rows", "pos"), scatter_dimension=1, tiled=True),
        lax.psum_scatter(short_w_grad, ("rows", "pos"), scatter_dimension=2, tiled=True),
        lax.psum_scatter(short_b_grad, ("rows", "pos"), scatter_dimension=1, tiled=True),
        lax.psum_scatter(skip_grad, ("rows", "pos"), scatter_dimension=0, tiled=True),
        lax.psum_scatter(out_grad_w, ("rows", "pos"), scatter_dimension=0, tiled=True),
        lax.psum_scatter(out_bias_grad, ("rows", "pos"), scatter_dimension=0, tiled=True),
        lax.psum_scatter(post_gain_grad, ("rows", "pos"), scatter_dimension=0, tiled=True),
        lax.psum_scatter(post_bias_grad, ("rows", "pos"), scatter_dimension=0, tiled=True),
        lax.psum_scatter(up_grad, ("rows", "pos"), scatter_dimension=0, tiled=True),
        lax.psum_scatter(up_bias_grad, ("rows", "pos"), scatter_dimension=0, tiled=True),
        lax.psum_scatter(down_grad, ("rows", "pos"), scatter_dimension=0, tiled=True),
        lax.psum_scatter(down_bias_grad, ("rows", "pos"), scatter_dimension=0, tiled=True),
        lax.psum_scatter(three_grad, ("rows", "pos"), scatter_dimension=1, tiled=True),
    )
    inner_sum = lax.psum(
        (inner_grads[0], inner_grads[1], inner_grads[2], inner_grads[3], inner_grads[4]),
        ("rows", "pos"),
    )
    return (
        result.astype(half),
        input_grad,
        summed[0],
        summed[1],
        summed[2],
        summed[3],
        summed[4],
        summed[5],
        summed[6],
        summed[7],
        summed[8],
        summed[9],
        summed[10],
        summed[11],
        summed[12],
        summed[13],
        summed[14],
        inner_sum[0],
        inner_sum[1],
        inner_sum[2],
        inner_sum[3],
        inner_sum[4],
        summed[15],
    )


def solution(mesh):
    return jax.shard_map(
        on_device,
        mesh=mesh,
        in_specs=(
            P("rows", "pos", None),
            P("rows", "pos", None),
            P("rows", None),
            P("rows", None),
            P(("rows", "pos")),
            P(("rows", "pos")),
            P(("rows", "pos"), None, None),
            P(None, ("rows", "pos")),
            P(None, None, ("rows", "pos")),
            P(None, ("rows", "pos")),
            P(("rows", "pos")),
            P(("rows", "pos"), None),
            P(("rows", "pos")),
            P(("rows", "pos")),
            P(("rows", "pos")),
            P(("rows", "pos"), None),
            P(("rows", "pos")),
            P(("rows", "pos"), None),
            P(("rows", "pos")),
            P(),
            P(),
            P(),
            P(),
            P(),
            P(None, ("rows", "pos")),
        ),
        out_specs=(
            P("rows", "pos", None),
            P("rows", "pos", None),
            P(("rows", "pos")),
            P(("rows", "pos")),
            P(("rows", "pos"), None, None),
            P(None, ("rows", "pos")),
            P(None, None, ("rows", "pos")),
            P(None, ("rows", "pos")),
            P(("rows", "pos")),
            P(("rows", "pos"), None),
            P(("rows", "pos")),
            P(("rows", "pos")),
            P(("rows", "pos")),
            P(("rows", "pos"), None),
            P(("rows", "pos")),
            P(("rows", "pos"), None),
            P(("rows", "pos")),
            P(),
            P(),
            P(),
            P(),
            P(),
            P(None, ("rows", "pos")),
        ),
        check_vma=False,
    )
```

profile of v0, /device:TPU:0, one launch (start us, length us, event | category | flops | bytes accessed | tf_op | source)
XLA Modules:
  0.0 3118.1 jit_solution(7585186939673742897)
XLA Ops:
  11.4 72.7 %all_gather.54 = bf16[64,1024]{0,1:T(8,128)(2,1)S(1)} all-gather(bf16[64,32]{0,1:T(8,128)(2,1)} %param.49), channel_id=1, replica_groups=mesh['rows'=8,'pos'=4] {'rows','pos'}, dimensions={1}, use_global_device_ids=true | all-gather | bytes 135168 | tf_op jit(solution)/shard_map/all_gather | solution.py:213
  95.7 52.2 %all-reduce.26 = (bf16[1024]{0:T(1024)(128)(2,1)S(1)}, bf16[1024]{0:T(1024)(128)(2,1)S(1)}, bf16[1024]{0:T(1024)(128)(2,1)S(1)}, bf16[1024]{0:T(1024)(128)(2,1)}...) all-reduce(bf16[1024]{0:T(1024)(128)(2,1)S(1)} %dynamic-update-slic, ...), channel_id=1, replica_groups=mesh['rows'=8,'pos'=4] {'rows','pos'}, use_global_device_ids=true, to_apply=%add.11 | all-reduce | flops 7168 | bytes 28672
  147.9 67.3 %all-gather.1 = bf16[32,32,3]{1,2,0:T(4,128)(2,1)S(1)} all-gather(bf16[1,32,3]{1,2,0:T(4,128)(2,1)S(1)} %bitcast.1166), channel_id=1, replica_groups=mesh['rows'=8,'pos'=4] {'rows','pos'}, dimensions={0}, use_global_device_ids=true | all-gather | bytes 6336 | tf_op jit(solution)/shard_map/all_gather | solution.py:201
  237.7 102.0 %all-gather = bf16[32,32,3]{1,2,0:T(4,128)(2,1)S(1)} all-gather(bf16[1,32,3]{1,2,0:T(4,128)(2,1)S(1)} %bitcast.1167), channel_id=1, replica_groups=mesh['rows'=8,'pos'=4] {'rows','pos'}, dimensions={0}, use_global_device_ids=true | all-gather | bytes 6336 | tf_op jit(solution)/shard_map/all_gather | solution.py:203
  340.8 69.9 %all_gather.49 = bf16[3,3,1024]{1,0,2:T(4,128)(2,1)S(1)} all-gather(bf16[3,3,32]{1,0,2:T(4,128)(2,1)S(1)} %copy.599), channel_id=1, replica_groups=mesh['rows'=8,'pos'=4] {'rows','pos'}, dimensions={2}, use_global_device_ids=true | all-gather | bytes 19008 | tf_op jit(solution)/shard_map/all_gather | solution.py:202
  434.5 9.0 multiply_add_fusion
  473.7 20.1 fusion.128
  493.8 8.7 fusion.178
  579.9 23.3 multiply_add_fusion.11
  640.8 16.9 fusion.112
  692.9 11.7 copy.1065
  705.2 10.6 reduce.31
  721.8 67.0 %all-gather.2 = bf16[32,1,128]{2,1,0:T(2,128)(2,1)S(1)} all-gather(bf16[1,1,128]{2,1,0:T(2,128)(2,1)S(1)} %bitcast.1169), channel_id=1, replica_groups=mesh['rows'=8,'pos'=4] {'rows','pos'}, dimensions={0}, use_global_device_ids=true | all-gather | bytes 8448 | tf_op jit(solution)/shard_map/all_gather | solution.py:210
  798.7 10.8 fusion.959
  809.6 14.0 fusion.968
  843.1 12.4 all_to_all.74
  878.6 10.6 fusion.391
  895.4 10.8 fusion.381
  920.3 10.6 fusion.385
  930.9 10.6 fusion.387
  941.5 11.2 fusion.250
  952.7 12.0 fusion.238
  964.7 10.6 fusion.235
  975.3 11.0 fusion.244
  986.3 10.6 fusion.241
  996.9 34.7 %multiply_add_fusion.2 = (f32[64,256,64]{1,2,0:T(8,128)}, f32[64,256,64]{1,2,0:T(8,128)}, f32[64,256,64]{1,2,0:T(8,128)}, f32[64,256,64]{1,2,0:T(8,128)}, f32[64...) fusion(f32[64,256,64]{1,2,0:T(8,128)} %get-tuple-element.141, ...), kind=kOutput, calls=%fused_computation.215 | convolution fusion | flops 453042176 | bytes 100696064 | tf_op jit(solution)/shard_map/transpose(jvp(qm,bkqc->bkmc))/dot_general | solution.py:103
  1091.1 13.1 fusion.11
  1104.2 15.7 fusion.350
  1126.0 19.8 fusion.60
  1145.8 14.5 add_bitcast_fusion.2
  1163.0 16.9 fusion.41
  1179.9 14.9 add_bitcast_fusion.1
  1197.4 16.7 fusion.22
  1214.1 18.2 add_bitcast_fusion
  1249.8 17.6 copy.707
  1290.5 27.2 all-to-all-done.4
  1359.6 8.7 fusion.954
  1369.6 15.6 fusion.361
  1386.8 10.8 fusion.290
  1398.2 12.2 fusion.272
  1411.8 129.9 %reduce-scatter.27.cloned.1.call-done = f32[32,9]{1,0:T(8,128)} async-done(((f32[1024,9]{1,0:T(8,128)}), f32[32,9]{1,0:T(8,128)}) %reduce-scatter.27.cloned.1.call-update) | async-done | bytes 1168
  1543.3 130.9 %reduce-scatter.25.cloned.1.call-done = f32[32,3]{1,0:T(8,128)} async-done(((f32[1024,3]{1,0:T(8,128)}), f32[32,3]{1,0:T(8,128)}) %reduce-scatter.25.cloned.1.call-update) | async-done | bytes 400
  1675.5 153.7 %all-reduce.29.cloned.1.call-done = (f32[1024]{0:T(1024)}, f32[1024]{0:T(1024)}, f32[1024]{0:T(1024)}, f32[1024]{0:T(1024)}, f32[1024]{0:T(1024)}, /*index=5*/f3...) async-done(((f32[1024]{0:T(1024)}, f32[1024]{0:T(1024)}, ...) | async-done | bytes 70672
  1839.3 130.6 %reduce-scatter.23.cloned.1.call-done = f32[64,32]{0,1:T(8,128)} async-done(((f32[64,1024]{0,1:T(8,128)}), f32[64,32]{0,1:T(8,128)}) %reduce-scatter.23.cloned.1.call-update) | async-done | bytes 8208 | tf_op jit(solution)/shard_map/reduce_scatter | solution.py:348
  1969.9 140.4 %reduce-scatter.17.cloned.1.call-done = f32[32,1024]{1,0:T(8,128)} async-done(((f32[1024,1024]{1,0:T(8,128)}), f32[32,1024]{1,0:T(8,128)}) %reduce-scatter.17.cloned.1.call-update) | async-done | bytes 131088 | tf_op jit(solution)/shard_map/reduce_scatter | solution.py:340
  2110.3 270.9 %reduce-scatter.15.cloned.1.call-done = f32[32,3,1024]{2,0,1:T(8,128)} async-done(((f32[1024,3,1024]{2,0,1:T(8,128)}), f32[32,3,1024]{2,0,1:T(8,128)}) %reduce-scatter.15.cloned.1.call-update) | async-done | bytes 393232 | tf_op jit(solution)/shard_map/reduce_scatter | solution.py:335
  2381.1 361.9 %reduce-scatter.21.cloned.1.call-done = f32[128,1024]{1,0:T(8,128)} async-done(((f32[4096,1024]{1,0:T(8,128)}), f32[128,1024]{1,0:T(8,128)}) %reduce-scatter.21.cloned.1.call-update) | async-done | bytes 524304 | tf_op jit(solution)/shard_map/reduce_scatter | solution.py:346
  2743.1 361.9 %reduce-scatter.19.cloned.1.call-done = f32[32,4096]{1,0:T(8,128)} async-done(((f32[1024,4096]{1,0:T(8,128)}), f32[32,4096]{1,0:T(8,128)}) %reduce-scatter.19.cloned.1.call-update) | async-done | bytes 524304 | tf_op jit(solution)/shard_map/reduce_scatter | solution.py:344
  (576 shorter events, 497.9 us)
Async XLA Ops:
  7.2 78.9 %copy-start = (bf16[64,64]{1,0:T(8,128)(2,1)S(1)}, bf16[64,64]{1,0:T(8,128)(2,1)}, u32[]{:S(2)}) copy-start(bf16[64,64]{1,0:T(8,128)(2,1)} %param.46) | copy-start | bytes 24580
  7.2 208.8 %all-gather.8.cloned.1.call-start = ((), (), s32[]{:S(2)}) async-start(), calls=%async_computation.14 | async-start | bytes 6488064 | tf_op jit(solution)/shard_map/all_gather | solution.py:200
  7.9 787.1 %all-gather.10.cloned.1.call-start = ((), (), s32[]{:S(2)}) async-start(), calls=%async_computation.15 | async-start | bytes 2162688 | tf_op jit(solution)/shard_map/all_gather | solution.py:205
  8.7 790.0 %all-gather.12.cloned.1.call-start = ((), (), s32[]{:S(2)}) async-start(), calls=%async_computation.16 | async-start | bytes 8650752 | tf_op jit(solution)/shard_map/all_gather | solution.py:209
  10.1 78.6 %copy-start.107 = (f32[64]{0:T(128)}, f32[64]{0:T(128)S(1)}, u32[]{:S(2)}) copy-start(f32[64]{0:T(128)S(1)} %convert_element_type.579) | copy-start | bytes 772
  88.8 59.1 %copy-start.144 = (bf16[3,32]{1,0:T(4,128)(2,1)S(1)}, bf16[3,32]{1,0:T(4,128)(2,1)}, u32[]{:S(2)}) copy-start(bf16[3,32]{1,0:T(4,128)(2,1)} %param.32) | copy-start | bytes 580
  88.8 126.5 %copy-start.41 = (bf16[1,512,1024]{2,1,0:T(8,128)(2,1)S(1)}, bf16[1,512,1024]{2,1,0:T(8,128)(2,1)}, u32[]{:S(2)}) copy-start(bf16[1,512,1024]{2,1,0:T(8,128)(2,1)} %param.25) | copy-start | bytes 3145732
  90.4 141.2 %all-to-all-start.1 = ((f32[512,4,256]{2,0,1:T(8,128)}), f32[512,4,256]{2,0,1:T(8,128)S(1)}, u32[]{:S(2)}, u32[]{:S(2)}) async-start(f32[512,4,256]{2,0,1:T(8,128)} %bitcast.1117), calls=%async_computation.1 | async-start | bytes 4194304 | tf_op jit(solution)/shard_map/all_to_all | solution.py:241
  147.9 76.0 %copy-start.135 = (f32[1024]{0:T(1024)}, f32[1024]{0:T(1024)S(1)}, u32[]{:S(2)}) copy-start(f32[1024]{0:T(1024)S(1)} %convert_element_type.567) | copy-start | bytes 12292
  147.9 76.0 %copy-start.92 = (f32[1024]{0:T(1024)}, f32[1024]{0:T(1024)S(1)}, u32[]{:S(2)}) copy-start(f32[1024]{0:T(1024)S(1)} %convert_element_type.566) | copy-start | bytes 12292
  231.6 179.7 %copy-start.146 = (s32[1,3]{1,0:T(1,128)S(1)}, s32[1,3]{1,0:T(1,128)}, u32[]{:S(2)}) copy-start(s32[1,3]{1,0:T(1,128)} %param.27) | copy-start | bytes 40
  231.6 189.8 %all-to-all-start = ((bf16[1,512,3,1024]{1,2,0,3:T(4,128)(2,1)}), bf16[1,512,3,1024]{1,2,0,3:T(4,128)(2,1)}, u32[]{:S(2)}, u32[]{:S(2)}) async-start(bf16[1,512,3,1024]{1,2,0,3:T(4,128)(2,1)} %copy.602), calls=%async_computation | async-start | bytes 8388608 | tf_op jit(solution)/shard_map/all_to_all | solution.py:250
  236.6 573.0 %all-gather.14.cloned.1.call-start = ((), (), s32[]{:S(2)}) async-start(), calls=%async_computation.17 | async-start | bytes 8650752 | tf_op jit(solution)/shard_map/all_gather | solution.py:211
  237.3 102.7 %copy-start.96 = (pred[2048]{0:T(1024)(128)(4,1)}, pred[2048]{0:T(1024)(128)(4,1)S(1)}, u32[]{:S(2)}) copy-start(pred[2048]{0:T(1024)(128)(4,1)S(1)} %get-tuple-element.37) | copy-start | bytes 6148
  237.3 102.7 %copy-start.99 = (pred[2048]{0:T(1024)(128)(4,1)}, pred[2048]{0:T(1024)(128)(4,1)S(1)}, u32[]{:S(2)}) copy-start(pred[2048]{0:T(1024)(128)(4,1)S(1)} %get-tuple-element.38) | copy-start | bytes 6148
  237.3 102.7 %copy-start.102 = (pred[2048]{0:T(1024)(128)(4,1)}, pred[2048]{0:T(1024)(128)(4,1)S(1)}, u32[]{:S(2)}) copy-start(pred[2048]{0:T(1024)(128)(4,1)S(1)} %get-tuple-element.39) | copy-start | bytes 6148
  237.4 209.5 %copy-start.78 = (pred[32,64]{1,0:T(8,128)(4,1)}, pred[32,64]{1,0:T(8,128)(4,1)S(1)}, u32[]{:S(2)}) copy-start(pred[32,64]{1,0:T(8,128)(4,1)S(1)} %broadcast_in_dim.205) | copy-start | bytes 6148
  237.5 209.4 %copy-start.88 = (pred[32,64]{1,0:T(8,128)(4,1)}, pred[32,64]{1,0:T(8,128)(4,1)S(1)}, u32[]{:S(2)}) copy-start(pred[32,64]{1,0:T(8,128)(4,1)S(1)} %broadcast_in_dim.197) | copy-start | bytes 6148
  237.5 209.3 %copy-start.90 = (pred[32,64]{1,0:T(8,128)(4,1)}, pred[32,64]{1,0:T(8,128)(4,1)S(1)}, u32[]{:S(2)}) copy-start(pred[32,64]{1,0:T(8,128)(4,1)S(1)} %broadcast_in_dim.202) | copy-start | bytes 6148
  411.1 23.4 copy-start.82
  411.1 23.4 copy-start.84
  411.2 23.3 copy-start.86
  411.4 23.1 copy-start.94
  411.4 23.1 copy-start.115
  411.4 23.1 copy-start.117
  717.5 71.4 %all-to-all-start.2 = ((bf16[4,2,65536]{2,1,0:T(2,128)(2,1)}), bf16[4,2,65536]{2,1,0:T(2,128)(2,1)}, u32[]{:S(2)}, u32[]{:S(2)}) async-start(bf16[4,2,65536]{2,1,0:T(2,128)(2,1)} %reshape.1866), calls=%async_computation.2 | async-start | bytes 2097152 | tf_op jit(solution)/shard_map/all_to_all | solution.py:265
  721.8 107.3 %copy-start.128 = (f32[1024]{0:T(1024)}, f32[1024]{0:T(1024)S(1)}, u32[]{:S(2)}) copy-start(f32[1024]{0:T(1024)S(1)} %convert_element_type.589) | copy-start | bytes 12292
  721.8 76.9 %copy-start.137 = (f32[1024]{0:T(1024)}, f32[1024]{0:T(1024)S(1)}, u32[]{:S(2)}) copy-start(f32[1024]{0:T(1024)S(1)} %convert_element_type.590) | copy-start | bytes 12292
  798.3 30.8 copy-start.45
  798.3 30.7 copy-start.121
  798.7 30.4 copy-start.132
  867.4 74.1 %copy-start.1 = (f32[64,256,64]{1,2,0:T(8,128)}, f32[64,256,64]{1,2,0:T(8,128)S(1)}, u32[]{:S(2)}) copy-start(f32[64,256,64]{1,2,0:T(8,128)S(1)} %fusion.278) | copy-start | bytes 12582916
  870.4 71.0 %copy-start.2 = (f32[64,256,64]{1,2,0:T(8,128)}, f32[64,256,64]{1,2,0:T(8,128)S(1)}, u32[]{:S(2)}) copy-start(f32[64,256,64]{1,2,0:T(8,128)S(1)} %fusion.280) | copy-start | bytes 12582916
  1121.5 145.9 %all-to-all-start.5 = ((bf16[4,512,256]{2,1,0:T(8,128)(2,1)}), bf16[4,512,256]{2,1,0:T(8,128)(2,1)}, u32[]{:S(2)}, u32[]{:S(2)}) async-start(bf16[4,512,256]{2,1,0:T(8,128)(2,1)} %bitcast.262), calls=%async_computation.9 | async-start | bytes 2097152 | tf_op jit(solution)/shard_map/all_to_all | solution.py:324
  1197.3 37.9 %slice-start.2 = ((s8[6291456]{0:T(1024)(128)(4,1)}), s8[4194304]{0:T(1024)(128)(4,1)S(1)}, s32[]{:S(2)}) async-start(s8[6291456]{0:T(1024)(128)(4,1)} %bitcast.1100), calls=%async_computation.29 | async-start | bytes 8388608
  1214.1 21.3 copy-start.101
  1214.1 21.3 copy-start.104
  1214.1 21.3 copy-start.131
  1267.4 50.2 %all-to-all-start.4 = ((bf16[1,2048,3,256]{3,2,0,1:T(4,128)(2,1)}), bf16[1,2048,3,256]{3,2,0,1:T(4,128)(2,1)}, u32[]{:S(2)}, u32[]{:S(2)}) async-start(bf16[1,2048,3,256]{3,2,0,1:T(4,128)(2,1)} %copy.707), calls=%async_computation.4 | async-start | bytes 8388608 | tf_op jit(solution)/shard_map/all_to_all | solution.py:314
  1272.3 138.2 %reduce-scatter.29.cloned.1.call-start = ((), (), s32[]{:S(2)}) async-start(), calls=%async_computation.25 | async-start | bytes 540672
  1275.7 266.0 %reduce-scatter.27.cloned.1.call-start = ((), (), s32[]{:S(2)}) async-start(), calls=%async_computation.24 | async-start | bytes 540672
  1281.1 393.0 %reduce-scatter.25.cloned.1.call-start = ((), (), s32[]{:S(2)}) async-start(), calls=%async_computation.23 | async-start | bytes 540672
  1344.9 484.3 %all-reduce.29.cloned.1.call-start = ((), (), s32[]{:S(2)}) async-start(), calls=%async_computation.26 | async-start | bytes 199680
  1347.3 622.6 %reduce-scatter.23.cloned.1.call-start = ((), (), s32[]{:S(2)}) async-start(), calls=%async_computation.22 | async-start | bytes 540672 | tf_op jit(solution)/shard_map/reduce_scatter | solution.py:348
  1353.7 756.6 %reduce-scatter.17.cloned.1.call-start = ((), (), s32[]{:S(2)}) async-start(), calls=%async_computation.19 | async-start | bytes 4325376 | tf_op jit(solution)/shard_map/reduce_scatter | solution.py:340
  1358.4 1022.7 %reduce-scatter.15.cloned.1.call-start = ((), (), s32[]{:S(2)}) async-start(), calls=%async_computation.18 | async-start | bytes 12976128 | tf_op jit(solution)/shard_map/reduce_scatter | solution.py:335
  1368.4 1374.7 %reduce-scatter.21.cloned.1.call-start = ((), (), s32[]{:S(2)}) async-start(), calls=%async_computation.21 | async-start | bytes 17301504 | tf_op jit(solution)/shard_map/reduce_scatter | solution.py:346
  1385.2 1719.8 %reduce-scatter.19.cloned.1.call-start = ((), (), s32[]{:S(2)}) async-start(), calls=%async_computation.20 | async-start | bytes 17301504 | tf_op jit(solution)/shard_map/reduce_scatter | solution.py:344
  (131 other events, 840.2 us)
Sparse Core Ops, SparseCore 0:
  11.0 72.5 all-gather.7
  86.5 59.9 all-gather.9
  149.3 76.1 all-gather.11
  240.0 93.1 all-gather.13
  1275.9 133.4 reduce-scatter.28
  1411.5 130.2 reduce-scatter.26
  1544.0 130.0 reduce-scatter.24
  1682.3 146.8 all-reduce.28
  1834.8 135.0 reduce-scatter.22
  1972.6 137.6 reduce-scatter.16
  2113.2 267.9 reduce-scatter.14
  2383.9 359.1 reduce-scatter.20
  2745.9 359.0 reduce-scatter.18
where the time goes:
time: 3130 us; the launch traced here: 3120 us
  waiting for transfers between devices  1710 us (55%)
  matrix products  717 us (23%)
  blocking collectives  443 us (14%)
  local copies, waits for them, and re-layouts  132 us (4%)
  other arithmetic  75.7 us (2%)
    unnamed x17, waiting for transfers between devices  417 us
    reduce_scatter x1, waiting for transfers between devices, on_device(): lax.psum_scatter(up_grad, ('rows', 'pos'), scatter_dimension=0, tiled=True)  362 us
    reduce_scatter x1, waiting for transfers between devices, on_device(): lax.psum_scatter(down_grad, ('rows', 'pos'), scatter_dimension=0, tiled=T...  362 us
    reduce_scatter x1, waiting for transfers between devices, on_device(): lax.psum_scatter(in_grad_w, ('rows', 'pos'), scatter_dimension=0, tiled=T...  271 us
    reduce_scatter x1, waiting for transfers between devices, on_device(): lax.psum_scatter(out_grad_w, ('rows', 'pos'), scatter_dimension=0, tiled=...  140 us
    reduce_scatter x1, waiting for transfers between devices, on_device(): lax.psum_scatter(three_grad, ('rows', 'pos'), scatter_dimension=1, tiled=...  131 us
    all_gather x1, blocking collectives, on_device(): lax.all_gather(short_bias, ('rows', 'pos'), axis=1, tiled=True)  102 us
    dot_general x8, matrix products, spectrum(): jnp.einsum('kn,bnmc->bkmc', first_cos, blocks, precision=TRANSFORM_PRECIS...  102 us
  transfers between devices with their start and end apart: 18, of which 9 were waited for; matrix products, arithmetic and copies ran while one was open for 19% of the time, Pallas kernels for 0%

commit v1 on v0

v1 whole, which is shorter than its diff:
```python
import functools
import math

import jax
import jax.numpy as jnp
import ml_dtypes
import numpy as np
from jax import lax
from jax.experimental import pallas as pl
from jax.experimental.pallas import tpu as pltpu
from jax.sharding import Mesh
from jax.sharding import PartitionSpec as P

HIGHEST = lax.Precision.HIGHEST
F32 = jnp.float32
BF16 = jnp.bfloat16
BLOCK = 256
FREQ_CHUNK = 64
VMEM_LIMIT = 60 * 1024 * 1024


def layer_norm(values, norm_gain, norm_shift):
    centre = values - jnp.mean(values, axis=-1, keepdims=True)
    spread = jnp.mean(centre * centre, axis=-1, keepdims=True)
    return centre * lax.rsqrt(spread + 1e-05) * norm_gain + norm_shift


def positions_table(length, features):
    band_count = (features - 1) // 2
    places = np.arange(length, dtype=np.float64)
    ladder = 0.0001 + (band_count - 1 - 0.0001) * np.arange(band_count) / (band_count - 1)
    angles = 2.0 * math.pi / length * places[:, None] * ladder[None, :]
    table = np.concatenate(
        [places[:, None] / (length - 1), np.cos(angles), -np.sin(angles)], axis=1
    )
    return jnp.asarray(table.astype(np.float32))


def decay_of(length, channels, model_width):
    scaled = jnp.arange(length, dtype=F32) / (length - 1)
    slow_rate = math.log(0.01) / 1.5
    fast_rate = math.log(0.01) / 0.3
    rates = jnp.abs(slow_rate + (fast_rate - slow_rate) * channels / (model_width - 1))
    return jnp.exp(-scaled[:, None] * rates[None, :]) + 0.05


def filter_net(embedding, decay, w_one, b_one, w_two, b_two, frequency, w_three):
    layer_one = jnp.sin(frequency * (jnp.dot(embedding, w_one, precision=HIGHEST) + b_one))
    layer_two = jnp.sin(frequency * (jnp.dot(layer_one, w_two, precision=HIGHEST) + b_two))
    return jnp.dot(layer_two, w_three, precision=HIGHEST) * decay


def transform_tables():
    order = np.concatenate([np.arange(0, BLOCK, 2), np.arange(1, BLOCK, 2)])
    angle = math.pi / BLOCK * (order[:, None] + 0.5) * np.arange(BLOCK)[None, :]
    forward = np.concatenate([np.cos(angle), -np.sin(angle)], axis=0)
    tables = []
    for table in (forward, forward.T / BLOCK):
        high = table.astype(ml_dtypes.bfloat16)
        low = (table - high.astype(np.float64)).astype(ml_dtypes.bfloat16)
        tables.append(jnp.asarray(np.concatenate([high, high, low], axis=1)))
    return tables


def unit_table(bounds, length):
    docs = bounds.shape[0]
    units = length // BLOCK + docs - 1
    ends = jnp.concatenate([bounds[1:], jnp.full((1,), length, jnp.int32)])
    first = bounds // BLOCK
    count = jnp.where(ends > bounds, (ends - 1) // BLOCK - first + 1, 0)
    earlier = jnp.arange(docs)[:, None] >= jnp.arange(docs)[None, :]
    stops = jnp.sum(jnp.where(earlier, count[None, :], 0), axis=1)
    starts = stops - count
    unit = jnp.arange(units, dtype=jnp.int32)
    doc = jnp.sum((unit[:, None] >= stops[None, :]).astype(jnp.int32), axis=1)
    doc = jnp.minimum(doc, docs - 1)
    pick = (doc[:, None] == jnp.arange(docs)[None, :]).astype(jnp.int32)

    def of_doc(values):
        return jnp.sum(pick * values[None, :], axis=1)

    block = jnp.clip(of_doc(first - starts) + unit, 0, length // BLOCK - 1)
    return jnp.concatenate(
        [
            block,
            of_doc(bounds),
            of_doc(ends),
            of_doc(starts),
            of_doc(stops),
            starts,
            stops,
            bounds,
            stops[docs - 1 :],
        ]
    ).astype(jnp.int32)


class Units:
    def __init__(self, meta, length, docs):
        self.meta = meta
        self.docs = docs
        self.units = length // BLOCK + docs - 1

    def block(self, unit):
        return self.meta[unit]

    def low(self, unit):
        return self.meta[self.units + unit]

    def high(self, unit):
        return self.meta[2 * self.units + unit]

    def start(self, unit):
        return self.meta[3 * self.units + unit]

    def stop(self, unit):
        return self.meta[4 * self.units + unit]

    def doc_start(self, doc):
        return self.meta[5 * self.units + doc]

    def doc_stop(self, doc):
        return self.meta[5 * self.units + self.docs + doc]

    def bound(self, doc):
        return self.meta[5 * self.units + 2 * self.docs + doc]

    def total(self):
        return self.meta[5 * self.units + 3 * self.docs]

    def inside(self, unit, width):
        place = lax.broadcasted_iota(jnp.int32, (BLOCK, width), 0) + self.block(unit) * BLOCK
        return (place >= self.low(unit)) & (place < self.high(unit))


def rows_of(block):
    return pl.ds(pl.multiple_of(block * BLOCK, BLOCK), BLOCK)


def times(table, value):
    high = value.astype(BF16)
    low = (value - high.astype(F32)).astype(BF16)
    return jnp.dot(
        table[...], jnp.concatenate([high, low, high], axis=0), preferred_element_type=F32
    )


def tap_masks(units, block, width, ahead=0):
    place = lax.broadcasted_iota(jnp.int32, (BLOCK, width), 0) + (block * BLOCK + ahead)
    first = place == units.bound(0)
    second = place == units.bound(0) + 1
    for doc in range(1, units.docs):
        first = first | (place == units.bound(doc))
        second = second | (place == units.bound(doc) + 1)
    return jnp.logical_not(first), jnp.logical_not(first | second)


def delayed(ref, block):
    start = block * BLOCK
    here = ref[rows_of(block), :].astype(F32)
    before = ref[pl.ds(pl.multiple_of(jnp.maximum(start - 16, 0), 16), 16), :].astype(F32)
    joined = jnp.concatenate([before, here], axis=0)
    return (here, pltpu.roll(joined, 1, 0)[16:], pltpu.roll(joined, 2, 0)[16:])


def short_conv(parts, small, branch, masks):
    total = small[9 + branch : 10 + branch, :] + small[branch : branch + 1, :] * parts[0]
    total += jnp.where(masks[0], small[3 + branch : 4 + branch, :] * parts[1], 0.0)
    total += jnp.where(masks[1], small[6 + branch : 7 + branch, :] * parts[2], 0.0)
    return total


def mixer_forward_kernel(
    docs, meta, post, pre, val, filt, small, fwd, inv, branch, mixed, gated, spec, taps, prod
):
    length, width = gated.shape
    blocks = length // BLOCK
    units = Units(meta, length, docs)

    def gate(block, _):
        masks = tap_masks(units, block, width)
        part = short_conv(delayed(val, block), small, 2, masks)
        part *= short_conv(delayed(pre, block), small, 1, masks)
        gated[rows_of(block), :] = part
        mixed[rows_of(block), :] = small[12:13, :] * part
        taps[block] = times(fwd, filt[rows_of(block), :])
        return 0

    lax.fori_loop(0, blocks, gate, 0)

    def transform(unit, _):
        value = gated[rows_of(units.block(unit)), :]
        spec[unit] = times(fwd, jnp.where(units.inside(unit, width), value, 0.0))
        return 0

    lax.fori_loop(0, units.total(), transform, 0)

    def multiply(unit, _):
        for low in range(0, BLOCK, FREQ_CHUNK):
            re, im = pl.ds(low, FREQ_CHUNK), pl.ds(BLOCK + low, FREQ_CHUNK)

            def step(back, total):
                at = unit - back
                s_re, s_im, t_re, t_im = spec[at, re], spec[at, im], taps[back, re], taps[back, im]
                return (
                    total[0] + (s_re * t_re - s_im * t_im),
                    total[1] + (s_re * t_im + s_im * t_re),
                )

            zero = jnp.zeros((FREQ_CHUNK, width), F32)
            total = lax.fori_loop(0, unit - units.start(unit) + 1, step, (zero, zero))
            prod[unit, re] = total[0]
            prod[unit, im] = total[1]
        return 0

    lax.fori_loop(0, units.total(), multiply, 0)

    half = BLOCK // 2

    def bring_back(unit, _):
        last = jnp.maximum(unit - 1, 0)
        old = jnp.where(unit > units.start(unit), prod[last], 0.0)
        new = prod[unit]
        joined = jnp.concatenate(
            [
                new[:half] - old[BLOCK : BLOCK + half],
                new[half:BLOCK] + old[BLOCK + half :],
                new[BLOCK : BLOCK + half] + old[:half],
                new[BLOCK + half :] - old[half:BLOCK],
            ],
            axis=0,
        )
        value = times(inv, joined)
        rows = rows_of(units.block(unit))
        mixed[rows, :] += jnp.where(units.inside(unit, width), value, 0.0)
        return 0

    lax.fori_loop(0, units.total(), bring_back, 0)

    def finish(block, _):
        masks = tap_masks(units, block, width)
        gate_value = short_conv(delayed(post, block), small, 0, masks)
        branch[rows_of(block), :] = (gate_value * mixed[rows_of(block), :]).astype(BF16)
        return 0

    lax.fori_loop(0, blocks, finish, 0)


def mixer_backward_kernel(
    docs,
    meta,
    post,
    pre,
    val,
    filt,
    small,
    fwd,
    inv,
    mixed,
    branch_grad,
    proj_grad,
    filt_grad,
    sums,
    gated,
    gm,
    conv_grad,
    spec,
    taps,
    prod,
):
    length, width = gated.shape
    blocks = length // BLOCK
    units = Units(meta, length, docs)
    half = BLOCK // 2
    sums[...] = jnp.zeros_like(sums)

    def total_rows(value):
        return jnp.sum(value, axis=0, keepdims=True)

    def gate(block, _):
        rows = rows_of(block)
        masks = tap_masks(units, block, width)
        part = short_conv(delayed(val, block), small, 2, masks)
        part *= short_conv(delayed(pre, block), small, 1, masks)
        gated[rows, :] = part
        grad = branch_grad[rows, :].astype(F32)
        mix_grad = grad * short_conv(delayed(post, block), small, 0, masks)
        gm[rows, :] = mix_grad
        conv_grad[0, rows, :] = grad * mixed[rows, :]
        conv_grad[1, rows, :] = small[12:13, :] * mix_grad
        sums[15:16, :] += total_rows(part * mix_grad)
        taps[block] = times(fwd, filt[rows, :])
        return 0

    lax.fori_loop(0, blocks, gate, 0)

    def transform(unit, _):
        rows = rows_of(units.block(unit))
        inside = units.inside(unit, width)
        spec[unit] = times(fwd, jnp.where(inside, gated[rows, :], 0.0))
        prod[unit] = times(fwd, jnp.where(inside, gm[rows, :], 0.0))
        return 0

    lax.fori_loop(0, units.total(), transform, 0)

    def spread(unit, _):
        after = jnp.minimum(unit + 1, units.units - 1)
        new = jnp.where(unit + 1 < units.stop(unit), prod[after], 0.0)
        prod[unit, pl.ds(0, half)] += new[BLOCK : BLOCK + half]
        prod[unit, pl.ds(half, half)] -= new[BLOCK + half :]
        prod[unit, pl.ds(BLOCK, half)] -= new[:half]
        prod[unit, pl.ds(BLOCK + half, half)] += new[half:BLOCK]
        return 0

    lax.fori_loop(0, units.total(), spread, 0)

    def signal_grad(unit, _):
        pieces = []
        for low in range(0, BLOCK, FREQ_CHUNK):
            re, im = pl.ds(low, FREQ_CHUNK), pl.ds(BLOCK + low, FREQ_CHUNK)

            def step(ahead, total):
                at = unit + ahead
                g_re, g_im, t_re, t_im = (
                    prod[at, re],
                    prod[at, im],
                    taps[ahead, re],
                    taps[ahead, im],
                )
                return (
                    total[0] + (g_re * t_re + g_im * t_im),
                    total[1] + (g_im * t_re - g_re * t_im),
                )

            zero = jnp.zeros((FREQ_CHUNK, width), F32)
            pieces.append(lax.fori_loop(0, units.stop(unit) - unit, step, (zero, zero)))
        joined = jnp.concatenate([piece[0] for piece in pieces] + [piece[1] for piece in pieces])
        value = times(inv, joined)
        rows = rows_of(units.block(unit))
        conv_grad[1, rows, :] += jnp.where(units.inside(unit, width), value, 0.0)
        return 0

    lax.fori_loop(0, units.total(), signal_grad, 0)

    def tap_grad(back, _):
        pieces = []
        for low in range(0, BLOCK, FREQ_CHUNK):
            re, im = pl.ds(low, FREQ_CHUNK), pl.ds(BLOCK + low, FREQ_CHUNK)

            def step(unit, total):
                at = unit - back
                g_re, g_im, s_re, s_im = (
                    prod[unit, re],
                    prod[unit, im],
                    spec[at, re],
                    spec[at, im],
                )
                return (
                    total[0] + (g_re * s_re + g_im * s_im),
                    total[1] + (g_im * s_re - g_re * s_im),
                )

            zero = jnp.zeros((FREQ_CHUNK, width), F32)
            total = (zero, zero)
            for doc in range(docs):
                total = lax.fori_loop(
                    units.doc_start(doc) + back, units.doc_stop(doc), step, total
                )
            pieces.append(total)
        joined = jnp.concatenate([piece[0] for piece in pieces] + [piece[1] for piece in pieces])
        filt_grad[rows_of(back), :] = times(inv, joined)
        return 0

    lax.fori_loop(0, blocks, tap_grad, 0)

    def conv_back(block, _):
        rows = rows_of(block)
        masks = tap_masks(units, block, width)
        val_parts, pre_parts, post_parts = (
            delayed(val, block),
            delayed(pre, block),
            delayed(post, block),
        )
        gated_grad = conv_grad[1, rows, :]
        pre_grad = gated_grad * short_conv(val_parts, small, 2, masks)
        val_grad = gated_grad * short_conv(pre_parts, small, 1, masks)
        post_grad = conv_grad[0, rows, :]
        conv_grad[1, rows, :] = pre_grad
        conv_grad[2, rows, :] = val_grad
        for branch, (grad, parts) in enumerate(
            ((post_grad, post_parts), (pre_grad, pre_parts), (val_grad, val_parts))
        ):
            sums[branch : branch + 1, :] += total_rows(grad * parts[0])
            sums[3 + branch : 4 + branch, :] += total_rows(
                jnp.where(masks[0], grad * parts[1], 0.0)
            )
            sums[6 + branch : 7 + branch, :] += total_rows(
                jnp.where(masks[1], grad * parts[2], 0.0)
            )
            sums[9 + branch : 10 + branch, :] += total_rows(grad)
        return 0

    lax.fori_loop(0, blocks, conv_back, 0)

    def spread_taps(block, _):
        start = block * BLOCK
        one, _two = tap_masks(units, block, width, 1)
        _one, two = tap_masks(units, block, width, 2)
        place = lax.broadcasted_iota(jnp.int32, (BLOCK, width), 0) + start
        one = one & (place + 1 < length)
        two = two & (place + 2 < length)
        for branch in range(3):
            here = conv_grad[branch, rows_of(block), :]
            after = conv_grad[
                branch, pl.ds(pl.multiple_of(jnp.minimum(start + BLOCK, length - 8), 8), 8), :
            ]
            joined = jnp.concatenate([here, after], axis=0)
            size = BLOCK + 8
            next_one = pltpu.roll(joined, size - 1, 0)[:BLOCK]
            next_two = pltpu.roll(joined, size - 2, 0)[:BLOCK]
            total = small[branch : branch + 1, :] * here
            total += jnp.where(one, small[3 + branch : 4 + branch, :] * next_one, 0.0)
            total += jnp.where(two, small[6 + branch : 7 + branch, :] * next_two, 0.0)
            rounded = total.astype(BF16)
            proj_grad[rows_of(block), branch * width : (branch + 1) * width] = rounded
            sums[12 + branch : 13 + branch, :] += total_rows(rounded.astype(F32))
        return 0

    lax.fori_loop(0, blocks, spread_taps, 0)


def whole_spec(shape, column=0):
    return pl.BlockSpec(shape, lambda i, meta: (0, column), pipeline_mode=pl.Buffered(1))


def mixer_forward(meta, docs, projected, filt, small, tables):
    length, width = filt.shape
    units = length // BLOCK + docs - 1
    column = [whole_spec((length, width), at) for at in range(3)]
    return pl.pallas_call(
        functools.partial(mixer_forward_kernel, docs),
        out_shape=(
            jax.ShapeDtypeStruct((length, width), BF16),
            jax.ShapeDtypeStruct((length, width), F32),
        ),
        grid_spec=pltpu.PrefetchScalarGridSpec(
            num_scalar_prefetch=1,
            grid=(1,),
            in_specs=column
            + [whole_spec(value.shape) for value in (filt, small, tables[0], tables[1])],
            out_specs=(column[0], column[0]),
            scratch_shapes=[
                pltpu.VMEM((length, width), F32),
                pltpu.VMEM((units, 2 * BLOCK, width), F32),
                pltpu.VMEM((length // BLOCK, 2 * BLOCK, width), F32),
                pltpu.VMEM((units, 2 * BLOCK, width), F32),
            ],
        ),
        compiler_params=pltpu.CompilerParams(vmem_limit_bytes=VMEM_LIMIT),
        cost_estimate=pl.CostEstimate(
            flops=40 * 10**9, bytes_accessed=10 * 10**6, transcendentals=0
        ),
        name="mixer_forward",
    )(meta, projected, projected, projected, filt, small, *tables)


def mixer_backward(meta, docs, projected, filt, small, tables, mixed, branch_grad):
    length, width = filt.shape
    units = length // BLOCK + docs - 1
    column = [whole_spec((length, width), at) for at in range(3)]
    return pl.pallas_call(
        functools.partial(mixer_backward_kernel, docs),
        out_shape=(
            jax.ShapeDtypeStruct((length, 3 * width), BF16),
            jax.ShapeDtypeStruct((length, width), F32),
            jax.ShapeDtypeStruct((16, width), F32),
        ),
        grid_spec=pltpu.PrefetchScalarGridSpec(
            num_scalar_prefetch=1,
            grid=(1,),
            in_specs=column
            + [
                whole_spec(value.shape)
                for value in (filt, small, tables[0], tables[1], mixed, branch_grad)
            ],
            out_specs=(
                whole_spec((length, 3 * width)),
                column[0],
                whole_spec((16, width)),
            ),
            scratch_shapes=[
                pltpu.VMEM((length, width), F32),
                pltpu.VMEM((length, width), F32),
                pltpu.VMEM((3, length, width), F32),
                pltpu.VMEM((units, 2 * BLOCK, width), F32),
                pltpu.VMEM((length // BLOCK, 2 * BLOCK, width), F32),
                pltpu.VMEM((units, 2 * BLOCK, width), F32),
            ],
        ),
        compiler_params=pltpu.CompilerParams(vmem_limit_bytes=VMEM_LIMIT),
        cost_estimate=pl.CostEstimate(
            flops=80 * 10**9, bytes_accessed=16 * 10**6, transcendentals=0
        ),
        name="mixer_backward",
    )(meta, projected, projected, projected, filt, small, *tables, mixed, branch_grad)


def norm_parts(values):
    centre = values - jnp.mean(values, axis=-1, keepdims=True)
    spread = jnp.mean(centre * centre, axis=-1, keepdims=True)
    scale = lax.rsqrt(spread + 1e-05)
    return centre * scale, scale


def project_kernel(inputs, norm, weight, bias, out):
    unit, _ = norm_parts(inputs[...].astype(F32))
    normed = (unit * norm[0:1, :] + norm[1:2, :]).astype(BF16)
    total = jnp.dot(normed, weight[...], preferred_element_type=F32) + bias[...]
    out[...] = total.astype(BF16)


def project(inputs, norm, weight, bias):
    length, depth = inputs.shape
    width = weight.shape[1]
    return pl.pallas_call(
        project_kernel,
        out_shape=jax.ShapeDtypeStruct((length, width), BF16),
        grid=(length // BLOCK,),
        in_specs=[
            pl.BlockSpec((BLOCK, depth), lambda i: (i, 0)),
            pl.BlockSpec(norm.shape, lambda i: (0, 0)),
            pl.BlockSpec(weight.shape, lambda i: (0, 0)),
            pl.BlockSpec(bias.shape, lambda i: (0, 0)),
        ],
        out_specs=pl.BlockSpec((BLOCK, width), lambda i: (i, 0)),
        compiler_params=pltpu.CompilerParams(vmem_limit_bytes=VMEM_LIMIT),
        cost_estimate=pl.CostEstimate(
            flops=2 * length * depth * width, bytes_accessed=10 * 10**6, transcendentals=0
        ),
        name="project",
    )(inputs, norm, weight, bias)


def project_back_kernel(inputs, norm, weight, grad, normed_grad, weight_grad, sums, total):
    @pl.when(pl.program_id(0) == 0)
    def _():
        total[...] = jnp.zeros_like(total)
        sums[...] = jnp.zeros_like(sums)

    unit, _ = norm_parts(inputs[...].astype(F32))
    normed = (unit * norm[0:1, :] + norm[1:2, :]).astype(BF16)
    cotangent = lax.dot_general(
        grad[...], weight[...], (((1,), (1,)), ((), ())), preferred_element_type=F32
    )
    normed_grad[...] = cotangent.astype(BF16)
    sums[0:1, :] += jnp.sum(cotangent * unit, axis=0, keepdims=True)
    sums[1:2, :] += jnp.sum(cotangent, axis=0, keepdims=True)
    total[...] += lax.dot_general(
        normed, grad[...], (((0,), (0,)), ((), ())), preferred_element_type=F32
    )

    @pl.when(pl.program_id(0) == pl.num_programs(0) - 1)
    def _():
        weight_grad[...] = total[...].astype(BF16)


def project_back(inputs, norm, weight, grad):
    length, depth = inputs.shape
    width = weight.shape[1]
    return pl.pallas_call(
        project_back_kernel,
        out_shape=(
            jax.ShapeDtypeStruct((length, depth), BF16),
            jax.ShapeDtypeStruct((depth, width), BF16),
            jax.ShapeDtypeStruct((8, depth), F32),
        ),
        grid=(length // BLOCK,),
        in_specs=[
            pl.BlockSpec((BLOCK, depth), lambda i: (i, 0)),
            pl.BlockSpec(norm.shape, lambda i: (0, 0)),
            pl.BlockSpec(weight.shape, lambda i: (0, 0)),
            pl.BlockSpec((BLOCK, width), lambda i: (i, 0)),
        ],
        out_specs=(
            pl.BlockSpec((BLOCK, depth), lambda i: (i, 0)),
            pl.BlockSpec((depth, width), lambda i: (0, 0)),
            pl.BlockSpec((8, depth), lambda i: (0, 0)),
        ),
        scratch_shapes=[pltpu.VMEM((depth, width), F32)],
        compiler_params=pltpu.CompilerParams(vmem_limit_bytes=VMEM_LIMIT),
        cost_estimate=pl.CostEstimate(
            flops=4 * length * depth * width, bytes_accessed=16 * 10**6, transcendentals=0
        ),
        name="project_back",
    )(inputs, norm, weight, grad)


def gelu_pair(u):
    root = math.sqrt(2.0 / math.pi)
    square = u * u
    curve = jnp.tanh(root * (u + 0.044715 * (u * square)))
    value = 0.5 * u * (1.0 + curve)
    slope = 0.5 * (1.0 + curve) + 0.5 * u * (1.0 - curve * curve) * (
        root * (1.0 + 3.0 * 0.044715 * square)
    )
    return value, slope


def feed_forward_kernel(
    normed_own,
    normed_other,
    grad_own,
    grad_other,
    up,
    up_bias,
    down,
    out_own,
    out_other,
    back_own,
    back_other,
    up_grad,
    down_grad,
    bias_grad,
    normed,
    grad,
    out_total,
    back_total,
):
    rows = normed_own.shape[0]
    at = pl.program_id(0)

    @pl.when(at == 0)
    def _():
        normed[:rows] = normed_own[...]
        normed[rows:] = normed_other[...]
        grad[:rows] = grad_own[...]
        grad[rows:] = grad_other[...]
        out_total[...] = jnp.zeros_like(out_total)
        back_total[...] = jnp.zeros_like(back_total)

    pre = jnp.dot(normed[...], up[...], preferred_element_type=F32) + up_bias[...]
    hidden, slope = gelu_pair(pre)
    hidden = hidden.astype(BF16)
    hidden_grad = lax.dot_general(
        grad[...], down[...], (((1,), (1,)), ((), ())), preferred_element_type=F32
    )
    pre_grad = hidden_grad * slope
    bias_grad[...] = jnp.sum(pre_grad, axis=0, keepdims=True)
    pre_grad = pre_grad.astype(BF16)
    out_total[...] += jnp.dot(hidden, down[...], preferred_element_type=F32)
    back_total[...] += lax.dot_general(
        pre_grad, up[...], (((1,), (1,)), ((), ())), preferred_element_type=F32
    )
    down_grad[...] = lax.dot_general(
        hidden, grad[...], (((0,), (0,)), ((), ())), preferred_element_type=F32
    ).astype(BF16)
    up_grad[...] = lax.dot_general(
        normed[...], pre_grad, (((0,), (0,)), ((), ())), preferred_element_type=F32
    ).astype(BF16)

    @pl.when(at == pl.num_programs(0) - 1)
    def _():
        out_own[...] = out_total[:rows]
        out_other[...] = out_total[rows:].astype(BF16)
        back_own[...] = back_total[:rows]
        back_other[...] = back_total[rows:].astype(BF16)


def feed_forward(normed_own, normed_other, grad_own, grad_other, up, up_bias, down):
    rows, depth = normed_own.shape
    width = up.shape[1]
    tile = 256
    fixed = pl.BlockSpec((rows, depth), lambda i: (0, 0), pipeline_mode=pl.Buffered(1))
    return pl.pallas_call(
        feed_forward_kernel,
        out_shape=(
            jax.ShapeDtypeStruct((rows, depth), F32),
            jax.ShapeDtypeStruct((rows, depth), BF16),
            jax.ShapeDtypeStruct((rows, depth), F32),
            jax.ShapeDtypeStruct((rows, depth), BF16),
            jax.ShapeDtypeStruct((depth, width), BF16),
            jax.ShapeDtypeStruct((width, depth), BF16),
            jax.ShapeDtypeStruct((1, width), F32),
        ),
        grid=(width // tile,),
        in_specs=[
            fixed,
            fixed,
            fixed,
            fixed,
            pl.BlockSpec((depth, tile), lambda i: (0, i)),
            pl.BlockSpec((1, tile), lambda i: (0, i)),
            pl.BlockSpec((tile, depth), lambda i: (i, 0)),
        ],
        out_specs=(
            fixed,
            fixed,
            fixed,
            fixed,
            pl.BlockSpec((depth, tile), lambda i: (0, i)),
            pl.BlockSpec((tile, depth), lambda i: (i, 0)),
            pl.BlockSpec((1, tile), lambda i: (0, i)),
        ),
        scratch_shapes=[
            pltpu.VMEM((2 * rows, depth), BF16),
            pltpu.VMEM((2 * rows, depth), BF16),
            pltpu.VMEM((2 * rows, depth), F32),
            pltpu.VMEM((2 * rows, depth), F32),
        ],
        compiler_params=pltpu.CompilerParams(vmem_limit_bytes=VMEM_LIMIT),
        cost_estimate=pl.CostEstimate(
            flops=12 * 2 * rows * depth * width,
            bytes_accessed=30 * 10**6,
            transcendentals=2 * rows * width,
        ),
        name="feed_forward",
    )(normed_own, normed_other, grad_own, grad_other, up, up_bias, down)


def swap(value, axis, bit):
    count = lax.axis_size(axis)
    return lax.ppermute(value, axis, [(at, at ^ bit) for at in range(count)])


def gather_halving(value, axis, bits):
    count = lax.axis_size(axis)
    me = lax.axis_index(axis)
    held = value[None]
    for bit in bits:
        held = jnp.concatenate([held, swap(held, axis, bit)], axis=0)
    order = [0]
    for bit in bits:
        order = order + [mask ^ bit for mask in order]
    place = {mask: at for at, mask in enumerate(order)}
    held = jnp.stack([held[place[mask]] for mask in range(count)])
    shape = held.shape
    bit = 1
    while bit < count:
        parts = held.reshape((count // (2 * bit), 2, bit) + shape[1:])
        held = jnp.where((me & bit) != 0, parts[:, ::-1], parts).reshape(shape)
        bit *= 2
    return held


def bits_of(count):
    return [1 << at for at in range(count.bit_length() - 1)]


def on_device(
    activations,
    out_grad,
    doc_bounds,
    doc_ids,
    pre_gain,
    pre_bias,
    in_weight,
    in_bias,
    short_weight,
    short_bias,
    skip_gain,
    out_weight,
    out_bias,
    post_gain,
    post_bias,
    up_weight,
    up_bias,
    down_weight,
    down_bias,
    filter_one,
    filter_bias_one,
    filter_two,
    filter_bias_two,
    filter_freq,
    filter_three,
):
    rz_count, pos_count = lax.axis_size("rz"), lax.axis_size("pos")
    pos, core = lax.axis_index("pos"), lax.axis_index("core")
    everything = ("rz", "core", "pos")
    owners = rz_count * 2 * pos_count
    own_at = (lax.axis_index("rz") * 2 + core) * pos_count + pos
    part_len, model_width = activations.shape[1:]
    length = part_len * pos_count
    own_width = pre_gain.shape[0]
    chan = model_width // pos_count
    ff_own = down_weight.shape[0]
    ff_half = rz_count * pos_count * ff_own
    docs = doc_bounds.shape[1]
    order = filter_two.shape[0]
    tables = transform_tables()
    meta = unit_table(doc_bounds[0], length)

    vectors = [
        pre_gain,
        pre_bias,
        out_bias,
        post_gain,
        post_bias,
        down_bias,
        skip_gain,
        in_bias,
        short_weight,
        short_bias,
        filter_three,
    ]
    small = jnp.concatenate(
        [value.reshape(-1, own_width) for value in vectors] + [up_bias.reshape(-1, own_width)]
    )
    small = lax.all_gather(small, "pos")
    small = lax.all_gather(small, "core")
    small = lax.all_gather(small, "rz").reshape(rz_count, 2, pos_count, -1, own_width)
    lines = small.transpose(3, 0, 1, 2, 4)
    lines = lines.reshape(-1, model_width).astype(F32)
    (
        pre_gain_all,
        pre_bias_all,
        out_bias_all,
        post_gain_all,
        post_bias_all,
        down_bias_all,
    ) = (lines[at] for at in range(6))
    up_lines = lines.shape[0] - ff_own // own_width
    up_bias_all = lines[up_lines:].reshape(ff_own // own_width, rz_count, 2, pos_count, own_width)
    up_bias_all = up_bias_all.transpose(2, 1, 3, 0, 4).reshape(2, ff_half)
    up_bias_half = lax.dynamic_index_in_dim(up_bias_all, core, 0)
    mine = lax.dynamic_slice_in_dim(lines[6:up_lines], pos * chan, chan, 1)
    proj_bias = mine[1:4].reshape(1, 3 * chan)
    taps = jnp.concatenate([mine[4:16], mine[0:1], jnp.zeros((3, chan), F32)])
    three = mine[16:]

    weight_in = in_weight.reshape(own_width, 3, pos_count, chan)
    weight_in = lax.all_to_all(weight_in, "pos", split_axis=2, concat_axis=0, tiled=True)
    weight_in = weight_in.reshape(pos_count * own_width, 3 * chan)
    weight_in = lax.all_gather(weight_in, ("rz", "core"), axis=0, tiled=True)

    up_parts = up_weight.reshape(own_width, rz_count, 2, pos_count * ff_own)
    up_keep = lax.dynamic_index_in_dim(up_parts, core, 2, False).reshape(own_width, ff_half)
    up_send = lax.dynamic_index_in_dim(up_parts, 1 - core, 2, False).reshape(own_width, ff_half)
    up_got = swap(up_send, "core", 1)
    up_pair = jnp.where(core == 0, jnp.stack([up_keep, up_got]), jnp.stack([up_got, up_keep]))
    up_all = lax.all_gather(up_pair, ("rz", "pos"))
    up_all = up_all.reshape(rz_count, pos_count, 2, own_width, ff_half)
    up_all = up_all.transpose(0, 2, 1, 3, 4).reshape(model_width, ff_half)
    down_all = lax.all_gather(down_weight, ("rz", "pos"), axis=0, tiled=True)
    out_all = lax.all_gather(out_weight, ("rz", "pos"))
    out_other = swap(out_all, "core", 1)
    out_all = jnp.where(
        core == 0, jnp.stack([out_all, out_other], 1), jnp.stack([out_other, out_all], 1)
    )
    out_all = out_all.reshape(rz_count, pos_count, 2, own_width, model_width)
    out_all = out_all.transpose(0, 2, 1, 3, 4).reshape(model_width, model_width)

    embedding = positions_table(length, filter_one.shape[0])
    channels = (pos * chan + jnp.arange(chan, dtype=jnp.int32)).astype(F32)
    decay = decay_of(length, channels, model_width)
    filt, filter_back = jax.vjp(
        functools.partial(filter_net, embedding, decay),
        filter_one.astype(F32),
        filter_bias_one.astype(F32),
        filter_two.astype(F32),
        filter_bias_two.astype(F32),
        filter_freq.astype(F32),
        three,
    )

    own_in = activations[0]
    bits = bits_of(pos_count)
    half = model_width // 2
    left = gather_halving(own_in[:, :half], "pos", bits)
    right = gather_halving(own_in[:, half:], "pos", bits[::-1])
    row_in = jnp.concatenate([left, right], axis=2).reshape(length, model_width)
    norm_one = jnp.stack([pre_gain_all, pre_bias_all])
    projected = project(row_in, norm_one, weight_in, proj_bias)
    branch, mixed = mixer_forward(meta, docs, projected, filt, taps, tables)
    branch_tokens = lax.all_to_all(
        branch.reshape(pos_count, part_len, chan), "pos", split_axis=0, concat_axis=0, tiled=True
    )
    branch_tokens = branch_tokens.transpose(1, 0, 2).reshape(part_len, model_width)

    inputs_f = own_in.astype(F32)
    residual = inputs_f + jnp.dot(branch_tokens, out_all, preferred_element_type=F32) + out_bias_all
    normed_two, post_back = jax.vjp(layer_norm, residual, post_gain_all, post_bias_all)
    normed_two = normed_two.astype(BF16)
    own_grad = out_grad[0]
    other_grad = swap(own_grad, "core", 1)
    ff_own_out, ff_other_out, back_own, back_other, up_grad, down_grad, up_bias_grad = feed_forward(
        normed_two,
        swap(normed_two, "core", 1),
        own_grad,
        other_grad,
        up_all,
        up_bias_half,
        down_all,
    )
    result = residual + (ff_own_out + swap(ff_other_out, "core", 1).astype(F32)) + down_bias_all
    result = result.astype(BF16)[None]
    grad_normed_two = back_own + swap(back_other, "core", 1).astype(F32)
    grad_out_f = own_grad.astype(F32)
    down_bias_grad = jnp.sum(grad_out_f, axis=0)
    grad_res_part, post_gain_grad, post_bias_grad = post_back(grad_normed_two)
    grad_residual = grad_out_f + grad_res_part
    out_bias_grad = jnp.sum(grad_residual, axis=0)
    grad_res_q = grad_residual.astype(BF16)
    branch_grad = lax.dot_general(
        grad_res_q, out_all, (((1,), (1,)), ((), ())), preferred_element_type=F32
    ).astype(BF16)
    branch_grad = lax.all_to_all(
        branch_grad.reshape(part_len, pos_count, chan).transpose(1, 0, 2),
        "pos",
        split_axis=0,
        concat_axis=0,
        tiled=True,
    ).reshape(length, chan)
    out_weight_grad = lax.dot_general(
        branch_tokens, grad_res_q, (((0,), (0,)), ((), ())), preferred_element_type=F32
    ).astype(BF16)

    def scatter(value, axes):
        return lax.psum_scatter(value, axes, scatter_dimension=0, tiled=False)

    out_parts = out_weight_grad.reshape(rz_count, 2, pos_count, own_width, model_width)
    out_keep = lax.dynamic_index_in_dim(out_parts, core, 1, False)
    out_send = lax.dynamic_index_in_dim(out_parts, 1 - core, 1, False)
    out_sum = (out_keep.astype(F32) + swap(out_send, "core", 1).astype(F32)).astype(BF16)
    up_parts = up_grad.reshape(rz_count, 2, pos_count, own_width, ff_half).transpose(0, 2, 1, 3, 4)
    bundle = jnp.concatenate(
        [
            up_parts.reshape(rz_count, pos_count, -1, model_width),
            down_grad.reshape(rz_count, pos_count, ff_own, model_width),
            out_sum,
        ],
        axis=2,
    ).transpose(1, 0, 2, 3)
    bundle = scatter(scatter(bundle, "pos"), "rz").astype(F32)
    up_rows = 2 * own_width * ff_half // model_width
    up_sum = bundle[:up_rows].reshape(2, own_width, ff_half)
    down_weight_grad = bundle[up_rows : up_rows + ff_own]
    out_weight_grad = bundle[up_rows + ff_own :]
    up_keep = lax.dynamic_index_in_dim(up_sum, core, 0, False)
    up_send = lax.dynamic_index_in_dim(up_sum, 1 - core, 0, False).astype(BF16)
    up_got = swap(up_send, "core", 1).astype(F32)
    up_pair = jnp.where(core == 0, jnp.stack([up_keep, up_got]), jnp.stack([up_got, up_keep]))
    up_weight_grad = up_pair.reshape(2, own_width, rz_count, pos_count * ff_own)
    up_weight_grad = up_weight_grad.transpose(1, 2, 0, 3).reshape(own_width, owners * ff_own)

    proj_grad, filt_grad, chan_sums = mixer_backward(
        meta, docs, projected, filt, taps, tables, mixed, branch_grad
    )
    normed_grad, weight_in_grad, pre_sums = project_back(row_in, norm_one, weight_in, proj_grad)
    normed_grad = scatter(
        normed_grad.reshape(pos_count, part_len, model_width), "pos"
    ).astype(F32)
    unit, scale = norm_parts(inputs_f)
    scaled = normed_grad * pre_gain_all
    grad_input = scale * (
        scaled
        - jnp.mean(scaled, axis=-1, keepdims=True)
        - unit * jnp.mean(scaled * unit, axis=-1, keepdims=True)
    )
    input_grad = (grad_residual + grad_input).astype(BF16)[None]
    weight_in_grad = scatter(
        weight_in_grad.reshape(rz_count * 2, pos_count * own_width, 3 * chan), ("rz", "core")
    )
    weight_in_grad = lax.all_to_all(
        weight_in_grad.reshape(pos_count, own_width, 3, chan),
        "pos",
        split_axis=0,
        concat_axis=0,
        tiled=True,
    )
    weight_in_grad = weight_in_grad.transpose(1, 2, 0, 3).reshape(own_width, 3, model_width)
    weight_in_grad = weight_in_grad.astype(F32)
    inner = filter_back(filt_grad)

    wide = jnp.concatenate([chan_sums, inner[5]])
    wide = lax.dynamic_update_slice_in_dim(
        jnp.zeros((wide.shape[0], model_width), F32), wide, pos * chan, 1
    )
    up_bias_wide = jnp.where(
        jnp.arange(2)[:, None] == core, jnp.broadcast_to(up_bias_grad, (2, ff_half)), 0.0
    )
    token_sums = jnp.stack(
        [
            pre_sums[0],
            pre_sums[1],
            out_bias_grad,
            post_gain_grad,
            post_bias_grad,
            down_bias_grad,
        ]
    )
    wide, up_bias_wide, token_sums, inner_sum = lax.psum(
        (wide, up_bias_wide, token_sums, tuple(inner[:5])), everything
    )
    wide = lax.dynamic_slice_in_dim(wide, own_at * own_width, own_width, 1)
    token_sums = lax.dynamic_slice_in_dim(token_sums, own_at * own_width, own_width, 1)
    up_bias_sum = up_bias_wide.reshape(2, rz_count, pos_count, ff_own)
    up_bias_sum = up_bias_sum.transpose(1, 0, 2, 3).reshape(-1)
    up_bias_sum = lax.dynamic_slice_in_dim(up_bias_sum, own_at * ff_own, ff_own, 0)
    return (
        result,
        input_grad,
        token_sums[0],
        token_sums[1],
        weight_in_grad,
        wide[12:15],
        wide[0:9].reshape(3, 3, own_width),
        wide[9:12],
        wide[15],
        out_weight_grad,
        token_sums[2],
        token_sums[3],
        token_sums[4],
        up_weight_grad,
        up_bias_sum,
        down_weight_grad,
        token_sums[5],
        *inner_sum,
        wide[16:],
    )


def solution(mesh):
    rows_count, pos_count = mesh.devices.shape
    fine = Mesh(mesh.devices.reshape(rows_count // 2, 2, pos_count), ("rz", "core", "pos"))
    rows = ("rz", "core")
    every = ("rz", "core", "pos")
    tokens = P(rows, "pos", None)
    vector = P(every)
    matrix = P(every, None)
    return jax.shard_map(
        on_device,
        mesh=fine,
        in_specs=(
            tokens,
            tokens,
            P(rows, None),
            P(rows, None),
            vector,
            vector,
            P(every, None, None),
            P(None, every),
            P(None, None, every),
            P(None, every),
            vector,
            matrix,
            vector,
            vector,
            vector,
            matrix,
            vector,
            matrix,
            vector,
            P(),
            P(),
            P(),
            P(),
            P(),
            P(None, every),
        ),
        out_specs=(
            tokens,
            tokens,
            vector,
            vector,
            P(every, None, None),
            P(None, every),
            P(None, None, every),
            P(None, every),
            vector,
            matrix,
            vector,
            vector,
            vector,
            matrix,
            vector,
            matrix,
            vector,
            P(),
            P(),
            P(),
            P(),
            P(),
            P(None, every),
        ),
        check_vma=False,
    )
```

time: 3130 us -> 915 us (0.29)
  waiting for transfers between devices: 1710 us -> 540 us
  matrix products: 717 us -> 34.4 us
  blocking collectives: 443 us -> 60.6 us
  Pallas kernels: 0 us -> 138 us
  local copies, waits for them, and re-layouts: 132 us -> 66 us
  other arithmetic: 75.7 us -> 42.6 us
    reduce_scatter x5 -> x2, waiting for transfers between devices: 1270 us -> 85.5 us  [scatter(): return lax.psum_scatter(value, axes, scatter_dimension=0, tiled=False)]
    dot_general x99 -> x6, matrix products: 712 us -> 21.3 us  [the longest x3 13.8 us: filter_net(): return jnp.dot(layer_two, w_three, precision=HIGHEST) * decay]
    all_gather x5 -> x3, blocking collectives: 379 us -> 31.9 us  [the longest x1 15.2 us: on_device(): lax.all_gather(small, 'rz').reshape(rz_count, 2, pos_count, -1, own_width)]
    unnamed x17 -> x12, waiting for transfers between devices: 417 us -> 96 us
    psum x0 -> x2, waiting for transfers between devices: none -> 251 us  [on_device(): lax.psum((wide, up_bias_wide, token_sums, tuple(inner[:5])), everything)]
    pallas_call x0 -> x5, Pallas kernels: none -> 138 us  [the longest x1 48.9 us: mixer_backward(): pl.pallas_call(functools.partial(mixer_backward_kernel, docs), out_shape=...]
    all_gather x4, waiting for transfers between devices: 0.04 us -> 78.1 us  [the longest x1 72.5 us: on_device(): down_all = lax.all_gather(down_weight, ('rz', 'pos'), axis=0, tiled=True)]
    unnamed x1 -> x0, blocking collectives: 52.2 us -> none
  transfers between devices with their start and end apart: 18 -> 24, of which waited for: 9 -> 13; matrix products, arithmetic and copies ran while one was open for 19% -> 14% of each run, Pallas kernels for 0% -> 4%
where the time goes in v1:
time: 915 us; the launch traced here: 909 us
  waiting for transfers between devices  540 us (59%)
  Pallas kernels  138 us (15%)
  local copies, waits for them, and re-layouts  66 us (7%)
  blocking collectives  60.6 us (7%)
  other arithmetic  42.6 us (5%)
  matrix products  34.4 us (4%)
  between operations  15.3 us (2%)
  starting transfers between devices  12.1 us (1%)
    psum x2, waiting for transfers between devices, on_device(): lax.psum((wide, up_bias_wide, token_sums, tuple(inner[:5])), everything)  251 us
    unnamed x12, waiting for transfers between devices  96 us
    reduce_scatter x2, waiting for transfers between devices, scatter(): return lax.psum_scatter(value, axes, scatter_dimension=0, tiled=False)  85.5 us
    all_gather x1, waiting for transfers between devices, on_device(): down_all = lax.all_gather(down_weight, ('rz', 'pos'), axis=0, tiled=True)  72.5 us
    pallas_call x1, Pallas kernels, mixer_backward(): pl.pallas_call(functools.partial(mixer_backward_kernel, docs), out_shape=...  48.9 us
    pallas_call x1, Pallas kernels, feed_forward(): pl.pallas_call(feed_forward_kernel, out_shape=(jax.ShapeDtypeStruct((rows...  40.2 us
    pallas_call x1, Pallas kernels, mixer_forward(): pl.pallas_call(functools.partial(mixer_forward_kernel, docs), out_shape=(...  25.2 us
    all_to_all x1, waiting for transfers between devices, on_device(): lax.all_to_all(branch.reshape(pos_count, part_len, chan), 'pos', split_ax...  20.8 us
  transfers between devices with their start and end apart: 24, of which 13 were waited for; matrix products, arithmetic and copies ran while one was open for 14% of the time, Pallas kernels for 4%

profile of v1, /device:TPU:0, one launch (start us, length us, event | category | flops | bytes accessed | tf_op | source)
XLA Modules:
  0.0 908.6 jit_solution(14946535302505193138)
XLA Ops:
  9.0 10.6 %all_to_all.30 = bf16[32,3,4,256]{3,0,1,2:T(8,128)(2,1)S(1)} all-to-all(bf16[32,3,4,256]{3,0,1,2:T(8,128)(2,1)S(1)} %bitcast.204), channel_id=1, replica_groups=mesh['rz'=4,'core'=2,'pos'=4] {'pos'}, dimensions={2} | all-to-all | bytes 393216 | tf_op jit(solution)/shard_map/all_to_all | solution.py:831
  28.6 14.8 %all-gather.4 = bf16[4,90,32]{1,2,0:T(8,128)(2,1)S(1)} all-gather(bf16[1,90,32]{1,2,0:T(8,128)(2,1)S(1)} %bitcast.215), channel_id=2, replica_groups=mesh['rz'=4,'core'=2,'pos'=4] {'pos'}, dimensions={0}, use_global_device_ids=true | all-gather | bytes 28800 | tf_op jit(solution)/shard_map/all_gather | solution.py:808
  43.4 1.8 all-gather.1
  45.3 15.2 %all-gather.2 = bf16[8,4,90,32]{2,3,1,0:T(8,128)(2,1)S(1)} all-gather(bf16[2,4,90,32]{2,3,1,0:T(8,128)(2,1)S(1)} %bitcast.209), channel_id=4, replica_groups=mesh['rz'=4,'core'=2,'pos'=4] {'rz'}, dimensions={0}, use_global_device_ids=true | all-gather | bytes 230400 | tf_op jit(solution)/shard_map/all_gather | solution.py:810
  64.1 2.0 copy.224
  67.4 2.0 convolution_add_fusion.1
  69.4 2.3 pad_maximum_fusion.4
  71.9 2.3 pad_maximum_fusion.3
  81.1 2.0 concatenate.63.meta
  83.7 2.8 convolution_add_fusion
  87.3 4.2 convolution_multiply_fusion.filt
  91.6 3.3 collective-permute-done.3
  97.7 1.7 pad_maximum_fusion.1
  102.7 2.5 pad_maximum_fusion.inputs
  105.2 10.4 %project.1.post.pre.val = bf16[2048,768]{1,0:T(8,128)(2,1)} custom-call(bf16[2048,1024]{1,0:T(8,128)(2,1)} %pad_maximum_fusion.inputs, f32[2,1024]{1,0:T(2,128)} %stack.69.norm, bf16[1024,768]{1,0:T(8,128)(2,1)} %all-gather.10.cloned.1.call-done.weight, f32[1,768]{1,0:T(1,128)} %bitcast.224), custom_call_target="tpu_custom_call" | custom-call | flops 3221225472 | bytes 10000000 | tf_op jit(solution)/shard_map/project/pallas_call | solution.py:525
  115.6 25.2 %mixer_forward.1 = (bf16[2048,256]{1,0:T(8,128)(2,1)}, f32[2048,256]{1,0:T(8,128)}) custom-call(s32[60]{0:T(128)} %concatenate.63.meta, bf16[2048,768]{1,0:T(8,128)(2,1)} %project.1.post.pre.val, bf16[2048,768]{1,0:T(8,128)(2,1)} %project.1.post.pre.val, bf16[2048,768]{1,0:T(8,128)(2,1)} %project.1.post.pre.val, f32[2048,256]{1,0:T(8,128)} %convolution_multiply_fusion.filt, ...), custom_call_target="tpu_custom_call" | custom-call | flops 40000000000 | bytes 10000000 | tf_op jit(solution)/shard_map/mixer_forward/pallas_call | solution.py:440
  140.8 2.4 copy.227
  143.1 4.3 all-to-all-start.1
  148.5 3.9 maximum_select_fusion
  152.3 20.8 %all-to-all-done.1 = bf16[4,512,256]{1,2,0:T(8,128)(2,1)} async-done(((bf16[4,512,256]{1,2,0:T(8,128)(2,1)}), bf16[4,512,256]{1,2,0:T(8,128)(2,1)}, u32[]{:S(2)}, u32[]{:S(2)}) %all-to-all-start.1) | async-done | bytes 1048608 | tf_op jit(solution)/shard_map/all_to_all | solution.py:874
  173.1 3.3 fusion.56
  179.0 5.6 all-gather.12.cloned.1.call-done
  184.6 4.8 copy.230
  189.4 72.5 %all-gather.14.cloned.1.call-done.down = bf16[2048,1024]{1,0:T(8,128)(2,1)} async-done(((bf16[128,1024]{1,0:T(8,128)(2,1)}), bf16[2048,1024]{1,0:T(8,128)(2,1)}) %all-gather.14.cloned.1.call-update) | async-done | bytes 4194320 | tf_op jit(solution)/shard_map/all_gather | solution.py:843
  261.9 40.2 %feed_forward.1 = (f32[512,1024]{1,0:T(8,128)}, bf16[512,1024]{1,0:T(8,128)(2,1)}, f32[512,1024]{1,0:T(8,128)}, bf16[512,1024]{1,0:T(8,128)(2,1)}, bf16[1024,204...) custom-call(bf16[512,1024]{1,0:T(8,128)(2,1)} %add_convert_fusion.1.normed_own, ...), custom_call_target="tpu_custom_call" | custom-call | flops 25769803776 | bytes 30000000 | tf_op jit(solution)/shard_map/feed_forward/pallas_call | solution.py:674
  302.7 2.4 collective-permute-done.9
  305.1 2.9 multiply_reduce_fusion
  308.3 3.8 fusion.52
  313.5 18.1 %all_to_all.31 = bf16[4,512,256]{2,1,0:T(8,128)(2,1)} all-to-all(bf16[4,512,256]{2,1,0:T(8,128)(2,1)S(1)} %bitcast.185), channel_id=1, replica_groups=mesh['rz'=4,'core'=2,'pos'=4] {'pos'}, dimensions={0} | all-to-all | bytes 2097152 | tf_op jit(solution)/shard_map/all_to_all | solution.py:906
  331.6 48.9 %mixer_backward.1 = (bf16[2048,768]{1,0:T(8,128)(2,1)}, f32[2048,256]{1,0:T(8,128)}, f32[16,256]{1,0:T(8,128)}) custom-call(s32[60]{0:T(128)} %concatenate.63.meta, bf16[2048,768]{1,0:T(8,128)(2,1)} %project.1.post.pre.val, bf16[2048,768]{1,0:T(8,128)(2,1)} %project.1.post.pre.val, bf16[2048,768]{1,0:T(8,128)(2,1)} %project.1.post.pre.val, ...), custom_call_target="tpu_custom_call" | custom-call | flops 80000000000 | bytes 16000000 | tf_op jit(solution)/shard_map/mixer_backward/pallas_call | solution.py:471
  380.5 13.4 %project_back.1 = (bf16[2048,1024]{1,0:T(8,128)(2,1)}, bf16[1024,768]{1,0:T(8,128)(2,1)}, f32[8,1024]{1,0:T(8,128)}) custom-call(bf16[2048,1024]{1,0:T(8,128)(2,1)} %pad_maximum_fusion.inputs, f32[2,1024]{1,0:T(2,128)} %stack.69.norm, bf16[1024,768]{1,0:T(8,128)(2,1)} %all-gather.10.cloned.1.call-done.weight, bf16[2048,768]{1,0:T(8,128)(2,1)} %get-tuple-element.44.grad), custom_call_target="tpu_custom_call" | custom-call | flops 6442450944 | bytes 16000000 | tf_op jit(solution)/shard_map/project_back/pallas_call | solution.py:570
  395.4 2.9 convolution_convert_fusion
  400.9 2.3 copy.237
  403.2 7.3 reshape.469
  410.9 7.5 maximum_bitcast_fusion
  421.1 4.9 fusion.18
  428.4 4.7 convolution_multiply_fusion.2
  433.1 3.0 fusion.33
  436.1 2.9 multiply_reduce_fusion.4
  439.0 2.4 fusion.31
  443.5 2.1 fusion.15
  445.7 2.3 convert_reduce_fusion.1
  448.7 93.2 %reduce-scatter.15.cloned.1.call-done = bf16[1,4,288,1024]{3,2,1,0:T(8,128)(2,1)} async-done(((bf16[4,4,288,1024]{3,2,1,0:T(8,128)(2,1)}), bf16[1,4,288,1024]{3,2,1,0:T(8,128)(2,1)}) %reduce-scatter.15.cloned.1.call-update) | async-done | bytes 2359312
  541.9 36.7 %reduce-scatter.9.cloned.1.call-done = bf16[1,128,768]{2,1,0:T(8,128)(2,1)} async-done(((bf16[8,128,768]{2,1,0:T(8,128)(2,1)}), bf16[1,128,768]{2,1,0:T(8,128)(2,1)}) %reduce-scatter.9.cloned.1.call-update) | async-done | bytes 196624 | tf_op jit(solution)/shard_map/reduce_scatter | solution.py:918
  580.2 3.5 all-to-all-start.3
  583.7 127.3 %all-reduce.6.cloned.1.call-done = f32[80,1024]{0,1:T(8,128)} async-done(((f32[80,1024]{0,1:T(8,128)}), f32[80,1024]{0,1:T(8,128)}) %all-reduce.6.cloned.1.call-update) | async-done | bytes 327696 | tf_op jit(solution)/shard_map/psum | solution.py:991
  718.3 123.4 %all-reduce.8.cloned.1.call-done = (f32[6,1024]{1,0:T(8,128)}, f32[4096]{0:T(1024)}, f32[33,64]{1,0:T(8,128)}, f32[64]{0:T(128)}, f32[64,64]{1,0:T(8,128)}, /*index=5*/f32[64]{0:T(128)}, f32[64]{0:T(128)}) async-done(((f32[6,1024]{1,0:T(8,128)}, f32[4096]{0:T(1024)}, f32[33,64]{1,0:T(8,128)}, f32[64]{0:T(128)}, f32[64,64]{1,0:T(8,128)}, /*index=5*/f32[64]{0:T(128)}, f32[64]{0:T(128)}), ...) | async-done | bytes 66576 | tf_op jit(solution)/shard_map/psum | solution.py:991
  844.2 48.8 %reduce-scatter.11.cloned.1.call-done = bf16[1,288,1024]{2,1,0:T(8,128)(2,1)} async-done(((bf16[4,288,1024]{2,1,0:T(8,128)(2,1)}), bf16[1,288,1024]{2,1,0:T(8,128)(2,1)}) %reduce-scatter.11.cloned.1.call-update) | async-done | bytes 589840 | tf_op jit(solution)/shard_map/reduce_scatter | solution.py:918
  (286 shorter events, 68.0 us)
Async XLA Ops:
  7.2 76.5 %copy-start = (bf16[64,64]{1,0:T(8,128)(2,1)S(1)}, bf16[64,64]{1,0:T(8,128)(2,1)}, u32[]{:S(2)}) copy-start(bf16[64,64]{1,0:T(8,128)(2,1)} %param.48) | copy-start | bytes 24580
  7.2 13.3 %copy-start.23 = (bf16[32,4096]{1,0:T(8,128)(2,1)S(1)}, bf16[32,4096]{1,0:T(8,128)(2,1)}, u32[]{:S(2)}) copy-start(bf16[32,4096]{1,0:T(8,128)(2,1)} %param.42) | copy-start | bytes 786436
  7.2 97.9 %all-gather.16.cloned.1.call-start = ((), (), s32[]{:S(2)}) async-start(), calls=%async_computation.14 | async-start | bytes 1114112 | tf_op jit(solution)/shard_map/all_gather | solution.py:844
  8.0 97.2 %all-gather.10.cloned.1.call-start = ((), (), s32[]{:S(2)}) async-start(), calls=%async_computation.8 | async-start | bytes 1769472 | tf_op jit(solution)/shard_map/all_gather | solution.py:833
  8.9 15.8 %copy-start.1 = (bf16[1,512,1024]{2,1,0:T(8,128)(2,1)S(1)}, bf16[1,512,1024]{2,1,0:T(8,128)(2,1)}, u32[]{:S(2)}) copy-start(bf16[1,512,1024]{2,1,0:T(8,128)(2,1)} %param.28) | copy-start | bytes 3145732
  20.5 164.1 %all-gather.12.cloned.1.call-start = ((), (), s32[]{:S(2)}) async-start(), calls=%async_computation.9 | async-start | bytes 4456448 | tf_op jit(solution)/shard_map/all_gather | solution.py:840
  20.7 6.1 copy-start.36
  20.7 6.5 copy-start.38
  20.8 6.6 copy-start.48
  20.8 6.8 copy-start.41
  20.8 6.9 copy-start.42
  20.8 6.9 copy-start.43
  20.8 7.0 copy-start.44
  20.8 7.1 copy-start.45
  22.6 1.4 collective-permute-start.7
  24.7 237.2 %all-gather.14.cloned.1.call-start = ((), (), s32[]{:S(2)}) async-start(), calls=%async_computation.10 | async-start | bytes 4456448 | tf_op jit(solution)/shard_map/all_gather | solution.py:843
  25.7 43.7 %collective-permute-start.2 = (bf16[1,512,512]{2,1,0:T(8,128)(2,1)S(1)}, bf16[1,512,512]{2,1,0:T(8,128)(2,1)}, u32[]{:S(2)}, u32[]{:S(2)}) collective-permute-start(bf16[1,512,512]{2,1,0:T(8,128)(2,1)S(1)} %get-tuple-element.230), channel_id=1, source_target_pairs={{0,2},{1,3},{2,0},{3,1},{4,6},{5,7},{6,4},{7,5},{8,10},{9,11},{10,... | collective-permute-start | bytes 1572872 | tf_op jit(solution)/shard_map/ppermute | solution.py:722
  26.4 45.5 %collective-permute-start = (bf16[1,512,512]{2,1,0:T(8,128)(2,1)}, bf16[1,512,512]{2,1,0:T(8,128)(2,1)}, u32[]{:S(2)}, u32[]{:S(2)}) collective-permute-start(bf16[1,512,512]{2,1,0:T(8,128)(2,1)} %get-tuple-element.229), channel_id=1, source_target_pairs={{0,1},{1,0},{2,3},{3,2},{4,5},{5,4},{6,7},{7,6},{8,9},{9,8},{10,11... | collective-permute-start | bytes 1572872 | tf_op jit(solution)/shard_map/ppermute | solution.py:722
  69.4 14.4 %copy-start.4 = (f32[2048,64]{0,1:T(8,128)}, f32[2048,64]{0,1:T(8,128)S(1)}, u32[]{:S(2)}) copy-start(f32[2048,64]{0,1:T(8,128)S(1)} %convolution_add_fusion.1) | copy-start | bytes 1572868
  69.4 8.3 slice-start
  71.7 7.8 copy-start.50
  71.7 7.8 copy-start.51
  71.7 23.2 %collective-permute-start.3 = (bf16[2,512,512]{2,1,0:T(8,128)(2,1)}, bf16[2,512,512]{2,1,0:T(8,128)(2,1)}, u32[]{:S(2)}, u32[]{:S(2)}) collective-permute-start(bf16[2,512,512]{2,1,0:T(8,128)(2,1)} %pad_maximum_fusion.4), channel_id=1, source_target_pairs={{0,1},{1,0},{2,3},{3,2},{4,5},{5,4},{6,7},{7,6},{8,9},{9,8},{10,11... | collective-permute-start | bytes 3145736 | tf_op jit(solution)/shard_map/ppermute | solution.py:722
  71.9 14.7 %copy-start.24 = (f32[2048]{0:T(1024)}, f32[2048]{0:T(1024)S(1)}, u32[]{:S(2)}) copy-start(f32[2048]{0:T(1024)S(1)} %multiply_negate_fusion) | copy-start | bytes 24580
  74.1 23.6 %collective-permute-start.1 = (bf16[2,512,512]{2,1,0:T(8,128)(2,1)}, bf16[2,512,512]{2,1,0:T(8,128)(2,1)}, u32[]{:S(2)}, u32[]{:S(2)}) collective-permute-start(bf16[2,512,512]{2,1,0:T(8,128)(2,1)} %pad_maximum_fusion.3), channel_id=1, source_target_pairs={{0,2},{1,3},{2,0},{3,1},{4,6},{5,7},{6,4},{7,5},{8,10},{9,11},{10,... | collective-permute-start | bytes 3145736 | tf_op jit(solution)/shard_map/ppermute | solution.py:722
  75.4 11.2 %copy-start.33 = (f32[256]{0:T(256)}, f32[256]{0:T(256)S(1)}, u32[]{:S(2)}) copy-start(f32[256]{0:T(256)S(1)} %add_abs_fusion) | copy-start | bytes 3076
  79.5 12.0 %copy-start.28 = (f32[64]{0:T(128)}, f32[64]{0:T(128)S(1)}, u32[]{:S(2)}) copy-start(f32[64]{0:T(128)S(1)} %convert_element_type.97) | copy-start | bytes 772
  81.0 10.6 %copy-start.22 = (bf16[80,4,2,4,32]{0,4,3,2,1:T(8,128)(2,1)}, bf16[80,4,2,4,32]{0,4,3,2,1:T(8,128)(2,1)S(1)}, u32[]{:S(2)}) copy-start(bf16[80,4,2,4,32]{0,4,3,2,1:T(8,128)(2,1)S(1)} %copy.226) | copy-start | bytes 491524
  105.2 43.3 %collective-permute-start.4 = (bf16[16,32,1024]{2,1,0:T(8,128)(2,1)}, bf16[16,32,1024]{2,1,0:T(8,128)(2,1)}, u32[]{:S(2)}, u32[]{:S(2)}) collective-permute-start(bf16[16,32,1024]{2,1,0:T(8,128)(2,1)} %bitcast.195), channel_id=1, source_target_pairs={{0,4},{4,0},{1,5},{5,1},{2,6},{6,2},{3,7},{7,3},{8,12},{12,8},{9,1... | collective-permute-start | bytes 3145736 | tf_op jit(solution)/shard_map/ppermute | solution.py:722
  140.8 6.8 copy-start.12
  143.1 29.9 %all-to-all-start.1 = ((bf16[4,512,256]{1,2,0:T(8,128)(2,1)}), bf16[4,512,256]{1,2,0:T(8,128)(2,1)}, u32[]{:S(2)}, u32[]{:S(2)}) async-start(bf16[4,512,256]{1,2,0:T(8,128)(2,1)} %copy.227), calls=%async_computation.1 | async-start | bytes 2097152 | tf_op jit(solution)/shard_map/all_to_all | solution.py:874
  147.5 296.0 %reduce-scatter.13.cloned.1.call-start = ((), (), s32[]{:S(2)}) async-start(), calls=%async_computation.15 | async-start | bytes 5242880
  147.5 41.9 %collective-permute-start.6 = (bf16[512,1024]{1,0:T(8,128)(2,1)}, bf16[512,1024]{1,0:T(8,128)(2,1)}, u32[]{:S(2)}, u32[]{:S(2)}) collective-permute-start(bf16[512,1024]{1,0:T(8,128)(2,1)} %bitcast.193), channel_id=1, source_target_pairs={{0,4},{4,0},{1,5},{5,1},{2,6},{6,2},{3,7},{7,3},{8,12},{12,8},{9,1... | collective-permute-start | bytes 3145736 | tf_op jit(solution)/shard_map/ppermute | solution.py:722
  178.2 11.2 %collective-permute-start.5 = (bf16[512,1024]{1,0:T(8,128)(2,1)}, bf16[512,1024]{1,0:T(8,128)(2,1)}, u32[]{:S(2)}, u32[]{:S(2)}) collective-permute-start(bf16[512,1024]{1,0:T(8,128)(2,1)} %add_convert_fusion.1.normed_own), channel_id=1, source_target_pairs={{0,4},{4,0},{1,5},{5,1},{2,6},{6,2},{3,7},{7,3},{8,12},{12,8},{9,1... | collective-permute-start | bytes 3145736 | tf_op jit(solution)/shard_map/ppermute | solution.py:722
  302.1 3.1 collective-permute-start.9
  302.1 5.9 collective-permute-start.8
  393.9 148.0 %reduce-scatter.15.cloned.1.call-start = ((), (), s32[]{:S(2)}) async-start(), calls=%async_computation.16 | async-start | bytes 11796480
  399.6 10.9 %collective-permute-start.10 = (bf16[4,4,32,1024]{3,2,0,1:T(8,128)(2,1)}, bf16[4,4,32,1024]{3,2,0,1:T(8,128)(2,1)S(1)}, u32[]{:S(2)}, u32[]{:S(2)}) collective-permute-start(bf16[4,4,32,1024]{3,2,0,1:T(8,128)(2,1)} %bitcast.171), channel_id=1, source_target_pairs={{0,4},{4,0},{1,5},{5,1},{2,6},{6,2},{3,7},{7,3},{8,12},{12,8},{9,1... | collective-permute-start | bytes 3145736 | tf_op jit(solution)/shard_map/ppermute | solution.py:722
  418.4 160.1 %reduce-scatter.9.cloned.1.call-start = ((), (), s32[]{:S(2)}) async-start(), calls=%async_computation.11 | async-start | bytes 1769472 | tf_op jit(solution)/shard_map/reduce_scatter | solution.py:918
  419.2 291.9 %all-reduce.6.cloned.1.call-start = ((), (), s32[]{:S(2)}) async-start(), calls=%async_computation.12 | async-start | bytes 1048576 | tf_op jit(solution)/shard_map/psum | solution.py:991
  419.9 6.0 copy-start.31
  426.0 7.1 copy-start.5
  439.0 6.6 copy-start.8
  441.4 400.2 %all-reduce.8.cloned.1.call-start = ((), (), s32[]{:S(2)}) async-start(), calls=%async_computation.17 | async-start | bytes 207872 | tf_op jit(solution)/shard_map/psum | solution.py:991
  448.6 444.4 %reduce-scatter.11.cloned.1.call-start = ((), (), s32[]{:S(2)}) async-start(), calls=%async_computation.13 | async-start | bytes 2949120 | tf_op jit(solution)/shard_map/reduce_scatter | solution.py:918
  580.2 137.2 %all-to-all-start.3 = ((bf16[4,32,3,256]{3,1,2,0:T(8,128)(2,1)}), bf16[4,32,3,256]{3,1,2,0:T(8,128)(2,1)S(1)}, u32[]{:S(2)}, u32[]{:S(2)}) async-start(bf16[4,32,3,256]{3,1,2,0:T(8,128)(2,1)} %copy.233), calls=%async_computation.4 | async-start | bytes 393216 | tf_op jit(solution)/shard_map/all_to_all | solution.py:963
  894.3 2.1 collective-permute-start.11
  894.9 6.1 copy-start.52
  (32 other events, 107.0 us)
Sparse Core Ops, SparseCore 0:
  10.8 58.2 all-gather.15
  70.7 23.7 all-gather.9
  97.9 86.6 all-gather.11
  187.2 74.6 all-gather.13
  394.0 49.4 reduce-scatter.12
  446.8 95.0 reduce-scatter.14
  544.2 34.2 reduce-scatter.8
  585.2 125.8 all-reduce.5
  718.6 122.9 all-reduce.7
  843.9 49.0 reduce-scatter.10

commit v2 on v1

--- a/solution.py
+++ b/solution.py
@@ -607,114 +607,162 @@
 
 
 def feed_forward_kernel(
+    masks,
+    place,
     normed_own,
     normed_other,
     grad_own,
     grad_other,
-    up,
     up_bias,
-    down,
-    out_own,
-    out_other,
-    back_own,
-    back_other,
-    up_grad,
-    down_grad,
-    bias_grad,
-    normed,
-    grad,
-    out_total,
-    back_total,
+    *rest,
 ):
-    rows = normed_own.shape[0]
-    at = pl.program_id(0)
-
-    @pl.when(at == 0)
-    def _():
-        normed[:rows] = normed_own[...]
-        normed[rows:] = normed_other[...]
-        grad[:rows] = grad_own[...]
-        grad[rows:] = grad_other[...]
-        out_total[...] = jnp.zeros_like(out_total)
-        back_total[...] = jnp.zeros_like(back_total)
-
-    pre = jnp.dot(normed[...], up[...], preferred_element_type=F32) + up_bias[...]
-    hidden, slope = gelu_pair(pre)
-    hidden = hidden.astype(BF16)
-    hidden_grad = lax.dot_general(
-        grad[...], down[...], (((1,), (1,)), ((), ())), preferred_element_type=F32
-    )
-    pre_grad = hidden_grad * slope
-    bias_grad[...] = jnp.sum(pre_grad, axis=0, keepdims=True)
-    pre_grad = pre_grad.astype(BF16)
-    out_total[...] += jnp.dot(hidden, down[...], preferred_element_type=F32)
-    back_total[...] += lax.dot_general(
-        pre_grad, up[...], (((1,), (1,)), ((), ())), preferred_element_type=F32
-    )
-    down_grad[...] = lax.dot_general(
-        hidden, grad[...], (((0,), (0,)), ((), ())), preferred_element_type=F32
-    ).astype(BF16)
-    up_grad[...] = lax.dot_general(
-        normed[...], pre_grad, (((0,), (0,)), ((), ())), preferred_element_type=F32
-    ).astype(BF16)
-
-    @pl.when(at == pl.num_programs(0) - 1)
-    def _():
-        out_own[...] = out_total[:rows]
-        out_other[...] = out_total[rows:].astype(BF16)
-        back_own[...] = back_total[:rows]
-        back_other[...] = back_total[rows:].astype(BF16)
-
-
-def feed_forward(normed_own, normed_other, grad_own, grad_other, up, up_bias, down):
+    count = 2 * len(masks)
+    pieces, rest = rest[:count], rest[count:]
+    out_own, out_other, back_own, back_other, bias_grad = rest[:5]
+    piece_grads, rest = rest[5 : 5 + count], rest[5 + count :]
+    normed, grad, out_total, back_total, weights, grads, load_sems, store_sems = rest
     rows, depth = normed_own.shape
-    width = up.shape[1]
-    tile = 256
-    fixed = pl.BlockSpec((rows, depth), lambda i: (0, 0), pipeline_mode=pl.Buffered(1))
+    tiles, pos_count, units, own_width, width = weights.shape
+    half = tiles // 2
+    columns = depth // width
+    down_units = (units - 2 * tiles) // columns
+    loads = [
+        (normed_own, normed.at[pl.ds(0, rows)]),
+        (normed_other, normed.at[pl.ds(rows, rows)]),
+        (grad_own, grad.at[pl.ds(0, rows)]),
+        (grad_other, grad.at[pl.ds(rows, rows)]),
+    ]
+    stores = []
+    for at, mask in enumerate(masks):
+        origin = jnp.bitwise_xor(place[0], mask)
+        for side in range(2):
+            part = pl.ds(side * half, half)
+            loads.append((pieces[2 * at + side], weights.at[part, origin]))
+            stores.append((grads.at[part, origin], piece_grads[2 * at + side]))
+    loads = [
+        pltpu.make_async_copy(source, target, load_sems.at[at])
+        for at, (source, target) in enumerate(loads)
+    ]
+    for copy in loads:
+        copy.start()
+    out_total[...] = jnp.zeros_like(out_total)
+    back_total[...] = jnp.zeros_like(back_total)
+    for copy in loads:
+        copy.wait()
+
+    def step(tile, _):
+        up = jnp.concatenate(
+            [
+                weights[block, :, side * tiles + tile].reshape(pos_count * own_width, width)
+                for block in range(tiles)
+                for side in range(2)
+            ],
+            axis=0,
+        )
+        down = jnp.concatenate(
+            [
+                weights[
+                    tile, :, 2 * tiles + at * down_units : 2 * tiles + (at + 1) * down_units
+                ].reshape(width, width)
+                for at in range(columns)
+            ],
+            axis=1,
+        )
+        pre = jnp.dot(normed[...], up, preferred_element_type=F32) + up_bias[pl.ds(tile, 1), :]
+        hidden, slope = gelu_pair(pre)
+        hidden = hidden.astype(BF16)
+        hidden_grad = lax.dot_general(
+            grad[...], down, (((1,), (1,)), ((), ())), preferred_element_type=F32
+        )
+        pre_grad = hidden_grad * slope
+        bias_grad[pl.ds(tile, 1), :] = jnp.sum(pre_grad, axis=0, keepdims=True)
+        pre_grad = pre_grad.astype(BF16)
+        out_total[...] += jnp.dot(hidden, down, preferred_element_type=F32)
+        back_total[...] += lax.dot_general(
+            pre_grad, up, (((1,), (1,)), ((), ())), preferred_element_type=F32
+        )
+        down_grad = lax.dot_general(
+            hidden, grad[...], (((0,), (0,)), ((), ())), preferred_element_type=F32
+        ).astype(BF16)
+        for at in range(columns):
+            grads[tile, :, 2 * tiles + at * down_units : 2 * tiles + (at + 1) * down_units] = (
+                down_grad[:, at * width : (at + 1) * width].reshape(
+                    pos_count, down_units, own_width, width
+                )
+            )
+        up_grad = lax.dot_general(
+            normed[...], pre_grad, (((0,), (0,)), ((), ())), preferred_element_type=F32
+        ).astype(BF16)
+        size = pos_count * own_width
+        for block in range(tiles):
+            for side in range(2):
+                low = (2 * block + side) * size
+                grads[block, :, side * tiles + tile] = up_grad[low : low + size].reshape(
+                    pos_count, own_width, width
+                )
+        return 0
+
+    lax.fori_loop(0, tiles, step, 0)
+    normed[:rows] = out_total[rows:].astype(BF16)
+    normed[rows:] = back_total[rows:].astype(BF16)
+    stores += [
+        (back_total.at[pl.ds(0, rows)], back_own),
+        (normed.at[pl.ds(rows, rows)], back_other),
+        (out_total.at[pl.ds(0, rows)], out_own),
+        (normed.at[pl.ds(0, rows)], out_other),
+    ]
+    stores = [
+        pltpu.make_async_copy(source, target, store_sems.at[at])
+        for at, (source, target) in enumerate(stores)
+    ]
+    for copy in stores:
+        copy.start()
+    for copy in stores:
+        copy.wait()
+
+
+def feed_forward(place, masks, normed_own, normed_other, grad_own, grad_other, up_bias, pieces):
+    rows, depth = normed_own.shape
+    tiles, width = up_bias.shape
+    piece = pieces[0].shape
+    whole = (tiles, len(masks)) + piece[1:]
+    anywhere = pl.BlockSpec(memory_space=pl.ANY)
+    bias = pl.BlockSpec((tiles, width), lambda i, place: (0, 0))
+    count = len(pieces)
     return pl.pallas_call(
-        feed_forward_kernel,
+        functools.partial(feed_forward_kernel, masks),
         out_shape=(
             jax.ShapeDtypeStruct((rows, depth), F32),
             jax.ShapeDtypeStruct((rows, depth), BF16),
             jax.ShapeDtypeStruct((rows, depth), F32),
             jax.ShapeDtypeStruct((rows, depth), BF16),
-            jax.ShapeDtypeStruct((depth, width), BF16),
-            jax.ShapeDtypeStruct((width, depth), BF16),
-            jax.ShapeDtypeStruct((1, width), F32),
-        ),
-        grid=(width // tile,),
-        in_specs=[
-            fixed,
-            fixed,
-            fixed,
-            fixed,
-            pl.BlockSpec((depth, tile), lambda i: (0, i)),
-            pl.BlockSpec((1, tile), lambda i: (0, i)),
-            pl.BlockSpec((tile, depth), lambda i: (i, 0)),
-        ],
-        out_specs=(
-            fixed,
-            fixed,
-            fixed,
-            fixed,
-            pl.BlockSpec((depth, tile), lambda i: (0, i)),
-            pl.BlockSpec((tile, depth), lambda i: (i, 0)),
-            pl.BlockSpec((1, tile), lambda i: (0, i)),
-        ),
-        scratch_shapes=[
-            pltpu.VMEM((2 * rows, depth), BF16),
-            pltpu.VMEM((2 * rows, depth), BF16),
-            pltpu.VMEM((2 * rows, depth), F32),
-            pltpu.VMEM((2 * rows, depth), F32),
-        ],
+            jax.ShapeDtypeStruct((tiles, width), F32),
+        )
+        + (jax.ShapeDtypeStruct(piece, BF16),) * count,
+        grid_spec=pltpu.PrefetchScalarGridSpec(
+            num_scalar_prefetch=1,
+            grid=(1,),
+            in_specs=[anywhere] * 4 + [bias] + [anywhere] * count,
+            out_specs=(anywhere,) * 4 + (bias,) + (anywhere,) * count,
+            scratch_shapes=[
+                pltpu.VMEM((2 * rows, depth), BF16),
+                pltpu.VMEM((2 * rows, depth), BF16),
+                pltpu.VMEM((2 * rows, depth), F32),
+                pltpu.VMEM((2 * rows, depth), F32),
+                pltpu.VMEM(whole, BF16),
+                pltpu.VMEM(whole, BF16),
+                pltpu.SemaphoreType.DMA((4 + count,)),
+                pltpu.SemaphoreType.DMA((4 + count,)),
+            ],
+        ),
         compiler_params=pltpu.CompilerParams(vmem_limit_bytes=VMEM_LIMIT),
         cost_estimate=pl.CostEstimate(
-            flops=12 * 2 * rows * depth * width,
+            flops=12 * 2 * rows * depth * width * tiles,
             bytes_accessed=30 * 10**6,
-            transcendentals=2 * rows * width,
+            transcendentals=2 * rows * width * tiles,
         ),
         name="feed_forward",
-    )(normed_own, normed_other, grad_own, grad_other, up, up_bias, down)
+    )(place, normed_own, normed_other, grad_own, grad_other, up_bias, *pieces)
 
 
 def swap(value, axis, bit):
@@ -740,6 +788,152 @@
         held = jnp.where((me & bit) != 0, parts[:, ::-1], parts).reshape(shape)
         bit *= 2
     return held
+
+
+def spread_pieces(own, bits):
+    held = {0: own}
+    for bit in bits:
+        held.update({mask ^ bit: swap(value, "pos", bit) for mask, value in list(held.items())})
+    return held
+
+
+def reduce_pieces(pieces, bits):
+    for bit in bits:
+        moved = {mask: swap(value, "pos", bit) for mask, value in pieces.items() if mask & bit}
+        pieces = {
+            mask: (value.astype(F32) + moved[mask ^ bit].astype(F32)).astype(BF16)
+            for mask, value in pieces.items()
+            if not mask & bit
+        }
+    return pieces[0]
+
+
+def reduce_line(chunks, axis):
+    count = lax.axis_size(axis)
+    me = lax.axis_index(axis)
+
+    def chunk(at):
+        return lax.dynamic_index_in_dim(chunks, jnp.clip(at, 0, count - 1), 0, False).astype(F32)
+
+    right = left = None
+    for step in range(1, count):
+        go_right = chunk(count - step + me)
+        go_left = chunk(step - count + me)
+        if step > 1:
+            go_right += right.astype(F32)
+            go_left += left.astype(F32)
+        right = lax.ppermute(
+            go_right.astype(BF16), axis, [(at, at + 1) for at in range(min(step, count - 1))]
+        )
+        left = lax.ppermute(
+            go_left.astype(BF16),
+            axis,
+            [(count - 1 - at, count - 2 - at) for at in range(min(step, count - 1))],
+        )
+    return chunk(me) + (right.astype(F32) + left.astype(F32))
+
+
+def small_sums_kernel(sizes, lines, send, total, shared, got, mine, send_sems, got_sems, share_sems, shared_sems):
+    rz_count, pos_count = sizes
+    owners = rz_count * 2 * pos_count
+    me = (lax.axis_index("rz") * 2 + lax.axis_index("core")) * pos_count + lax.axis_index("pos")
+
+    def device(at):
+        return (at // (2 * pos_count), (at // pos_count) % 2, at % pos_count)
+
+    barrier = pltpu.get_barrier_semaphore()
+
+    def greet(step, _):
+        pl.semaphore_signal(
+            barrier,
+            inc=1,
+            device_id=device((me + step) % owners),
+            device_id_type=pl.DeviceIdType.MESH,
+        )
+        return 0
+
+    lax.fori_loop(1, owners, greet, 0)
+    pl.semaphore_wait(barrier, owners - 1)
+
+    def part(step):
+        to = (me + step) % owners
+        return pltpu.make_async_remote_copy(
+            src_ref=send.at[to],
+            dst_ref=got.at[step],
+            send_sem=send_sems.at[step],
+            recv_sem=got_sems.at[step],
+            device_id=device(to),
+            device_id_type=pl.DeviceIdType.MESH,
+        )
+
+    def share(step):
+        to = (me + step) % owners
+        return pltpu.make_async_remote_copy(
+            src_ref=mine,
+            dst_ref=shared.at[me],
+            send_sem=share_sems.at[step],
+            recv_sem=shared_sems.at[step],
+            device_id=device(to),
+            device_id_type=pl.DeviceIdType.MESH,
+        )
+
+    def start(step, _):
+        part(step).start()
+        return 0
+
+    lax.fori_loop(1, owners, start, 0)
+    total[...] = send[me]
+
+    def add(step, _):
+        part(step).wait_recv()
+        total[...] += got[step]
+        return 0
+
+    lax.fori_loop(1, owners, add, 0)
+    mine[...] = total[lines:]
+    shared[me] = total[lines:]
+
+    def start_share(step, _):
+        share(step).start()
+        return 0
+
+    lax.fori_loop(1, owners, start_share, 0)
+
+    def finish(step, _):
+        part(step).wait_send()
+        share(step).wait()
+        return 0
+
+    lax.fori_loop(1, owners, finish, 0)
+
+
+def small_sums(sizes, send, lines):
+    owners, rows, _ = send.shape
+    return pl.pallas_call(
+        functools.partial(small_sums_kernel, sizes, lines),
+        out_shape=(
+            jax.ShapeDtypeStruct((rows, 128), F32),
+            jax.ShapeDtypeStruct((owners, rows - lines, 128), F32),
+        ),
+        in_specs=[pl.BlockSpec(memory_space=pltpu.VMEM)],
+        out_specs=(
+            pl.BlockSpec(memory_space=pltpu.VMEM),
+            pl.BlockSpec(memory_space=pltpu.VMEM),
+        ),
+        scratch_shapes=[
+            pltpu.VMEM((owners, rows, 128), F32),
+            pltpu.VMEM((rows - lines, 128), F32),
+            pltpu.SemaphoreType.DMA((owners,)),
+            pltpu.SemaphoreType.DMA((owners,)),
+            pltpu.SemaphoreType.DMA((owners,)),
+            pltpu.SemaphoreType.DMA((owners,)),
+        ],
+        compiler_params=pltpu.CompilerParams(
+            collective_id=0, has_side_effects=True, vmem_limit_bytes=32 * 1024 * 1024
+        ),
+        cost_estimate=pl.CostEstimate(flops=10**6, bytes_accessed=4 * 10**6, transcendentals=0),
+        name="small_sums",
+    )(send)
 
 
 def bits_of(count):
@@ -821,7 +1015,8 @@
     up_lines = lines.shape[0] - ff_own // own_width
     up_bias_all = lines[up_lines:].reshape(ff_own // own_width, rz_count, 2, pos_count, own_width)
     up_bias_all = up_bias_all.transpose(2, 1, 3, 0, 4).reshape(2, ff_half)
-    up_bias_half = lax.dynamic_index_in_dim(up_bias_all, core, 0)
+    up_bias_half = lax.dynamic_index_in_dim(up_bias_all, core, 0, False)
+    up_bias_half = up_bias_half.reshape(rz_count, pos_count * ff_own)
     mine = lax.dynamic_slice_in_dim(lines[6:up_lines], pos * chan, chan, 1)
     proj_bias = mine[1:4].reshape(1, 3 * chan)
     taps = jnp.concatenate([mine[4:16], mine[0:1], jnp.zeros((3, chan), F32)])
@@ -832,15 +1027,26 @@
     weight_in = weight_in.reshape(pos_count * own_width, 3 * chan)
     weight_in = lax.all_gather(weight_in, ("rz", "core"), axis=0, tiled=True)
 
-    up_parts = up_weight.reshape(own_width, rz_count, 2, pos_count * ff_own)
-    up_keep = lax.dynamic_index_in_dim(up_parts, core, 2, False).reshape(own_width, ff_half)
-    up_send = lax.dynamic_index_in_dim(up_parts, 1 - core, 2, False).reshape(own_width, ff_half)
-    up_got = swap(up_send, "core", 1)
-    up_pair = jnp.where(core == 0, jnp.stack([up_keep, up_got]), jnp.stack([up_got, up_keep]))
-    up_all = lax.all_gather(up_pair, ("rz", "pos"))
-    up_all = up_all.reshape(rz_count, pos_count, 2, own_width, ff_half)
-    up_all = up_all.transpose(0, 2, 1, 3, 4).reshape(model_width, ff_half)
-    down_all = lax.all_gather(down_weight, ("rz", "pos"), axis=0, tiled=True)
+    tile = pos_count * ff_own
+    columns = model_width // tile
+    bits = bits_of(pos_count)
+    orders = (bits, bits[::-1])
+    place = jnp.reshape(pos, (1,)).astype(jnp.int32)
+    up_parts = up_weight.reshape(own_width, rz_count, 2, tile).transpose(2, 1, 0, 3)
+    up_keep = lax.dynamic_index_in_dim(up_parts, core, 0, False)
+    up_got = swap(lax.dynamic_index_in_dim(up_parts, 1 - core, 0, False), "core", 1)
+    up_first = jnp.where(core == 0, up_keep, up_got)
+    up_second = jnp.where(core == 0, up_got, up_keep)
+    down_parts = down_weight.reshape(ff_own // own_width, own_width, columns, tile)
+    down_parts = down_parts.transpose(2, 0, 1, 3).reshape(-1, own_width, tile)
+    bundle = jnp.concatenate([up_first, up_second, down_parts])
+    bundle = lax.all_gather(bundle, "rz")
+    sides = [
+        spread_pieces(bundle[: rz_count // 2], orders[0]),
+        spread_pieces(bundle[rz_count // 2 :], orders[1]),
+    ]
+    masks = sorted(sides[0])
+    pieces = [sides[side][mask] for mask in masks for side in range(2)]
     out_all = lax.all_gather(out_weight, ("rz", "pos"))
     out_other = swap(out_all, "core", 1)
     out_all = jnp.where(
@@ -863,7 +1069,6 @@
     )
 
     own_in = activations[0]
-    bits = bits_of(pos_count)
     half = model_width // 2
     left = gather_halving(own_in[:, :half], "pos", bits)
     right = gather_halving(own_in[:, half:], "pos", bits[::-1])
@@ -882,14 +1087,15 @@
     normed_two = normed_two.astype(BF16)
     own_grad = out_grad[0]
     other_grad = swap(own_grad, "core", 1)
-    ff_own_out, ff_other_out, back_own, back_other, up_grad, down_grad, up_bias_grad = feed_forward(
+    ff_own_out, ff_other_out, back_own, back_other, up_bias_grad, *piece_grads = feed_forward(
+        place,
+        masks,
         normed_two,
         swap(normed_two, "core", 1),
         own_grad,
         other_grad,
-        up_all,
         up_bias_half,
-        down_all,
+        pieces,
     )
     result = residual + (ff_own_out + swap(ff_other_out, "core", 1).astype(F32)) + down_bias_all
     result = result.astype(BF16)[None]
@@ -917,30 +1123,40 @@
     def scatter(value, axes):
         return lax.psum_scatter(value, axes, scatter_dimension=0, tiled=False)
 
+    sums = [
+        reduce_pieces(
+            {mask: piece_grads[2 * at + side] for at, mask in enumerate(masks)}, orders[side]
+        )
+        for side in range(2)
+    ]
+    bundle = reduce_line(jnp.concatenate(sums), "rz")
+    up_sum = bundle[: 2 * rz_count].reshape(2, rz_count, own_width, tile)
+    up_keep = lax.dynamic_index_in_dim(up_sum, core, 0, False)
+    up_send = lax.dynamic_index_in_dim(up_sum, 1 - core, 0, False).astype(BF16)
+    up_got = swap(up_send, "core", 1).astype(F32)
+    up_pair = jnp.where(
+        core == 0, jnp.stack([up_keep, up_got], 1), jnp.stack([up_got, up_keep], 1)
+    )
+    up_weight_grad = up_pair.transpose(2, 0, 1, 3).reshape(own_width, owners * ff_own)
+    down_weight_grad = bundle[2 * rz_count :].reshape(columns, ff_own, tile)
+    down_weight_grad = down_weight_grad.transpose(1, 0, 2).reshape(ff_own, model_width)
+
     out_parts = out_weight_grad.reshape(rz_count, 2, pos_count, own_width, model_width)
     out_keep = lax.dynamic_index_in_dim(out_parts, core, 1, False)
     out_send = lax.dynamic_index_in_dim(out_parts, 1 - core, 1, False)
-    out_sum = (out_keep.astype(F32) + swap(out_send, "core", 1).astype(F32)).astype(BF16)
-    up_parts = up_grad.reshape(rz_count, 2, pos_count, own_width, ff_half).transpose(0, 2, 1, 3, 4)
-    bundle = jnp.concatenate(
+    out_sum = out_keep.astype(F32) + swap(out_send, "core", 1).astype(F32)
+    out_sum = jnp.stack(
         [
-            up_parts.reshape(rz_count, pos_count, -1, model_width),
-            down_grad.reshape(rz_count, pos_count, ff_own, model_width),
-            out_sum,
-        ],
-        axis=2,
-    ).transpose(1, 0, 2, 3)
-    bundle = scatter(scatter(bundle, "pos"), "rz").astype(F32)
-    up_rows = 2 * own_width * ff_half // model_width
-    up_sum = bundle[:up_rows].reshape(2, own_width, ff_half)
-    down_weight_grad = bundle[up_rows : up_rows + ff_own]
-    out_weight_grad = bundle[up_rows + ff_own :]
-    up_keep = lax.dynamic_index_in_dim(up_sum, core, 0, False)
-    up_send = lax.dynamic_index_in_dim(up_sum, 1 - core, 0, False).astype(BF16)
-    up_got = swap(up_send, "core", 1).astype(F32)
-    up_pair = jnp.where(core == 0, jnp.stack([up_keep, up_got]), jnp.stack([up_got, up_keep]))
-    up_weight_grad = up_pair.reshape(2, own_width, rz_count, pos_count * ff_own)
-    up_weight_grad = up_weight_grad.transpose(1, 2, 0, 3).reshape(own_width, owners * ff_own)
+            lax.dynamic_index_in_dim(out_sum, jnp.bitwise_xor(pos, mask), 1, False)
+            for mask in masks
+        ]
+    ).astype(BF16)
+    middle = rz_count // 2
+    out_sums = [
+        reduce_pieces({mask: out_sum[at, :middle] for at, mask in enumerate(masks)}, orders[0]),
+        reduce_pieces({mask: out_sum[at, middle:] for at, mask in enumerate(masks)}, orders[1]),
+    ]
+    out_weight_grad = reduce_line(jnp.concatenate(out_sums), "rz")
 
     proj_grad, filt_grad, chan_sums = mixer_backward(
         meta, docs, projected, filt, taps, tables, mixed, branch_grad
@@ -975,9 +1191,6 @@
     wide = lax.dynamic_update_slice_in_dim(
         jnp.zeros((wide.shape[0], model_width), F32), wide, pos * chan, 1
     )
-    up_bias_wide = jnp.where(
-        jnp.arange(2)[:, None] == core, jnp.broadcast_to(up_bias_grad, (2, ff_half)), 0.0
-    )
     token_sums = jnp.stack(
         [
             pre_sums[0],
@@ -988,14 +1201,36 @@
             down_bias_grad,
         ]
     )
-    wide, up_bias_wide, token_sums, inner_sum = lax.psum(
-        (wide, up_bias_wide, token_sums, tuple(inner[:5])), everything
-    )
-    wide = lax.dynamic_slice_in_dim(wide, own_at * own_width, own_width, 1)
-    token_sums = lax.dynamic_slice_in_dim(token_sums, own_at * own_width, own_width, 1)
-    up_bias_sum = up_bias_wide.reshape(2, rz_count, pos_count, ff_own)
-    up_bias_sum = up_bias_sum.transpose(1, 0, 2, 3).reshape(-1)
-    up_bias_sum = lax.dynamic_slice_in_dim(up_bias_sum, own_at * ff_own, ff_own, 0)
+    up_bias_wide = jnp.where(
+        jnp.arange(2)[None, :, None] == core, up_bias_grad.reshape(rz_count, 1, tile), 0.0
+    ).reshape(owners, ff_own)
+    by_owner = jnp.concatenate([token_sums, wide]).reshape(-1, owners, own_width)
+    count = by_owner.shape[0] * own_width
+    line_rows = -(-(count + ff_own) // 1024) * 8
+    by_owner = jnp.concatenate(
+        [
+            by_owner.transpose(1, 0, 2).reshape(owners, count),
+            up_bias_wide,
+            jnp.zeros((owners, line_rows * 128 - count - ff_own), F32),
+        ],
+        axis=1,
+    ).reshape(owners, line_rows, 128)
+    flat = jnp.concatenate([value.reshape(-1) for value in inner[:5]])
+    share = -(-flat.shape[0] // owners)
+    flat = jnp.pad(flat, (0, share * owners - flat.shape[0])).reshape(owners, share)
+    inner_rows = -(-share // 1024) * 8
+    flat = jnp.pad(flat, ((0, 0), (0, inner_rows * 128 - share)))
+    send = jnp.concatenate([by_owner, flat.reshape(owners, inner_rows, 128)], axis=1)
+    total, shared = small_sums((rz_count, pos_count), send, line_rows)
+    total = total[:line_rows].reshape(-1)
+    up_bias_sum = total[count : count + ff_own]
+    total = total[:count].reshape(-1, own_width)
+    token_sums, wide = total[:6], total[6:]
+    shared = shared.reshape(owners, inner_rows * 128)[:, :share].reshape(-1)
+    inner_sum, start = [], 0
+    for value in inner[:5]:
+        inner_sum.append(shared[start : start + value.size].reshape(value.shape))
+        start += value.size
     return (
         result,
         input_grad,

time: 915 us -> 592 us (0.65)
  waiting for transfers between devices: 540 us -> 146 us
  starting transfers between devices: 12.1 us -> 67.7 us
  Pallas kernels: 138 us -> 161 us
  blocking collectives: 60.6 us -> 44.5 us
  other arithmetic: 42.6 us -> 55 us
    psum x2 -> x0, waiting for transfers between devices: 251 us -> none  [on_device(): lax.psum((wide, up_bias_wide, token_sums, tuple(inner[:5])), everything)]
    ppermute x12 -> x30, waiting for transfers between devices: 8.55 us -> 133 us  [swap(): return lax.ppermute(value, axis, [(at, at ^ bit) for at in range(count)])]
    unnamed x12 -> x6, waiting for transfers between devices: 96 us -> 0.75 us
    reduce_scatter x2 -> x1, waiting for transfers between devices: 85.5 us -> 0.02 us  [scatter(): return lax.psum_scatter(value, axes, scatter_dimension=0, tiled=False)]
    all_gather x2 -> x1, waiting for transfers between devices: 78.1 us -> 0.01 us  [on_device(): bundle = lax.all_gather(bundle, 'rz')]
    ppermute x0 -> x12, starting transfers between devices: none -> 30.7 us  [the longest x6 24.4 us: reduce_line(): lax.ppermute(go_right.astype(BF16), axis, [(at, at + 1) for at in range(m...]
    pallas_call x1 -> x2, Pallas kernels: 40.2 us -> 63.5 us  [the longest x1 40.5 us: feed_forward(): pl.pallas_call(functools.partial(feed_forward_kernel, masks), out_shape=(...]
    ppermute x12 -> x30, starting transfers between devices: 3.3 us -> 25.8 us  [swap(): return lax.ppermute(value, axis, [(at, at ^ bit) for at in range(count)])]
  transfers between devices with their start and end apart: 24 -> 50, of which waited for: 13 -> 15; matrix products, arithmetic and copies ran while one was open for 14% -> 22% of each run, Pallas kernels for 4% -> 6%
where the time goes in v2:
time: 592 us; the launch traced here: 587 us
  Pallas kernels  161 us (27%)
  waiting for transfers between devices  146 us (25%)
  starting transfers between devices  67.7 us (11%)
  local copies, waits for them, and re-layouts  62.7 us (11%)
  other arithmetic  55 us (9%)
  blocking collectives  44.5 us (8%)
  matrix products  34.9 us (6%)
  between operations  15.3 us (3%)
    ppermute x30, waiting for transfers between devices, swap(): return lax.ppermute(value, axis, [(at, at ^ bit) for at in range(count)])  133 us
    pallas_call x1, Pallas kernels, mixer_backward(): pl.pallas_call(functools.partial(mixer_backward_kernel, docs), out_shape=...  48.8 us
    pallas_call x1, Pallas kernels, feed_forward(): pl.pallas_call(functools.partial(feed_forward_kernel, masks), out_shape=(...  40.5 us
    ppermute x30, starting transfers between devices, swap(): return lax.ppermute(value, axis, [(at, at ^ bit) for at in range(count)])  25.8 us
    pallas_call x1, Pallas kernels, mixer_forward(): pl.pallas_call(functools.partial(mixer_forward_kernel, docs), out_shape=(...  25.1 us
    ppermute x6, starting transfers between devices, reduce_line(): lax.ppermute(go_right.astype(BF16), axis, [(at, at + 1) for at in range(m...  24.4 us
    pallas_call x1, Pallas kernels, small_sums(): pl.pallas_call(functools.partial(small_sums_kernel, sizes, lines), out_sh...  23 us
    all_to_all x1, blocking collectives, on_device(): lax.all_to_all(branch_grad.reshape(part_len, pos_count, chan).transpose(1...  17.9 us
  transfers between devices with their start and end apart: 50, of which 15 were waited for; matrix products, arithmetic and copies ran while one was open for 22% of the time, Pallas kernels for 6%

profile of v2, /device:TPU:0, one launch (start us, length us, event | category | flops | bytes accessed | tf_op | source)
XLA Modules:
  0.0 586.7 jit_solution(5068174024708886733)
XLA Ops:
  9.5 3.0 collective-permute-start.2
  14.7 3.4 all-to-all-start
  21.7 10.1 %all-gather.5 = bf16[4,90,32]{1,2,0:T(8,128)(2,1)S(1)} all-gather(bf16[1,90,32]{1,2,0:T(8,128)(2,1)S(1)} %bitcast.314), channel_id=2, replica_groups=mesh['rz'=4,'core'=2,'pos'=4] {'pos'}, dimensions={0}, use_global_device_ids=true | all-gather | bytes 28800 | tf_op jit(solution)/shard_map/all_gather | solution.py:1002
  34.5 14.7 %all-gather.2 = bf16[8,4,90,32]{2,3,1,0:T(8,128)(2,1)S(1)} all-gather(bf16[2,4,90,32]{2,3,1,0:T(8,128)(2,1)S(1)} %bitcast.311), channel_id=4, replica_groups=mesh['rz'=4,'core'=2,'pos'=4] {'rz'}, dimensions={0}, use_global_device_ids=true | all-gather | bytes 230400 | tf_op jit(solution)/shard_map/all_gather | solution.py:1004
  73.7 4.9 convolution_multiply_fusion.filt
  81.2 2.8 collective-permute-done.3
  85.3 10.4 %collective-permute-done.1 = bf16[2,512,512]{2,1,0:T(8,128)(2,1)} collective-permute-done((bf16[2,512,512]{2,1,0:T(8,128)(2,1)}, bf16[2,512,512]{2,1,0:T(8,128)(2,1)}, u32[]{:S(2)}, u32[]{:S(2)}) %collective-permute-start.1) | collective-permute-done | bytes 1048608 | tf_op jit(solution)/shard_map/ppermute | solution.py:770
  99.4 2.5 pad_maximum_fusion.inputs
  102.0 10.3 %project.1.post.pre.val = bf16[2048,768]{1,0:T(8,128)(2,1)} custom-call(bf16[2048,1024]{1,0:T(8,128)(2,1)} %pad_maximum_fusion.inputs, f32[2,1024]{1,0:T(2,128)} %copy.311.norm, bf16[1024,768]{1,0:T(8,128)(2,1)} %all-gather.10.cloned.1.call-done.weight, f32[1,768]{1,0:T(1,128)} %bitcast.318), custom_call_target="tpu_custom_call" | custom-call | flops 3221225472 | bytes 10000000 | tf_op jit(solution)/shard_map/project/pallas_call | solution.py:525
  112.3 25.1 %mixer_forward.1 = (bf16[2048,256]{1,0:T(8,128)(2,1)}, f32[2048,256]{1,0:T(8,128)}) custom-call(s32[60]{0:T(128)} %concatenate.79.meta, bf16[2048,768]{1,0:T(8,128)(2,1)} %project.1.post.pre.val, bf16[2048,768]{1,0:T(8,128)(2,1)} %project.1.post.pre.val, bf16[2048,768]{1,0:T(8,128)(2,1)} %project.1.post.pre.val, f32[2048,256]{1,0:T(8,128)} %convolution_multiply_fusion.filt, ...), custom_call_target="tpu_custom_call" | custom-call | flops 40000000000 | bytes 10000000 | tf_op jit(solution)/shard_map/mixer_forward/pallas_call | solution.py:440
  137.3 2.3 copy.291
  139.6 3.6 all-to-all-start.1
  145.4 3.3 maximum_select_fusion
  148.7 3.1 fusion.97
  158.5 3.5 fusion.104
  163.8 16.3 %collective-permute-done.8.rest_2_ = bf16[2,16,32,512]{3,2,1,0:T(8,128)(2,1)} collective-permute-done((bf16[2,16,32,512]{3,2,1,0:T(8,128)(2,1)}, bf16[2,16,32,512]{3,2,1,0:T(8,128)(2,1)}, u32[]{:S(2)}, u32[]{:S(2)}) %collective-permute-start.8) | collective-permute-done | bytes 1048608 | tf_op jit(solution)/shard_map/ppermute | solution.py:770
  181.3 21.3 %collective-permute-done.11.rest_5_ = bf16[2,16,32,512]{3,2,1,0:T(8,128)(2,1)} collective-permute-done((bf16[2,16,32,512]{3,2,1,0:T(8,128)(2,1)}, bf16[2,16,32,512]{3,2,1,0:T(8,128)(2,1)}, u32[]{:S(2)}, u32[]{:S(2)}) %collective-permute-start.11) | collective-permute-done | bytes 1048608 | tf_op jit(solution)/shard_map/ppermute | solution.py:770
  204.2 20.1 %collective-permute-done.12.rest_6_ = bf16[2,16,32,512]{3,2,1,0:T(8,128)(2,1)} collective-permute-done((bf16[2,16,32,512]{3,2,1,0:T(8,128)(2,1)}, bf16[2,16,32,512]{3,2,1,0:T(8,128)(2,1)}, u32[]{:S(2)}, u32[]{:S(2)}) %collective-permute-start.12) | collective-permute-done | bytes 1048608 | tf_op jit(solution)/shard_map/ppermute | solution.py:770
  224.3 2.3 collective-permute-done.13.rest_7_
  226.6 40.5 %feed_forward.1 = (f32[512,1024]{1,0:T(8,128)}, bf16[512,1024]{1,0:T(8,128)(2,1)}, f32[512,1024]{1,0:T(8,128)}, bf16[512,1024]{1,0:T(8,128)(2,1)}, f32[4,512]{1,...) custom-call(s32[1]{0:T(128)} %bitcast.40.place, ...), custom_call_target="tpu_custom_call" | custom-call | flops 25769803776 | bytes 30000000 | tf_op jit(solution)/shard_map/feed_forward/pallas_call | solution.py:732
  267.8 2.4 collective-permute-done.15
  270.2 2.9 multiply_reduce_fusion
  273.4 3.8 fusion.96
  277.2 3.3 convolution_convert_fusion.1
  280.6 17.9 %all_to_all.30 = bf16[4,512,256]{2,1,0:T(8,128)(2,1)} all-to-all(bf16[4,512,256]{2,1,0:T(8,128)(2,1)S(1)} %bitcast.280), channel_id=1, replica_groups=mesh['rz'=4,'core'=2,'pos'=4] {'pos'}, dimensions={0} | all-to-all | bytes 2097152 | tf_op jit(solution)/shard_map/all_to_all | solution.py:1112
  298.4 48.8 %mixer_backward.1 = (bf16[2048,768]{1,0:T(8,128)(2,1)}, f32[2048,256]{1,0:T(8,128)}, f32[16,256]{1,0:T(8,128)}) custom-call(s32[60]{0:T(128)} %concatenate.79.meta, bf16[2048,768]{1,0:T(8,128)(2,1)} %project.1.post.pre.val, bf16[2048,768]{1,0:T(8,128)(2,1)} %project.1.post.pre.val, bf16[2048,768]{1,0:T(8,128)(2,1)} %project.1.post.pre.val, ...), custom_call_target="tpu_custom_call" | custom-call | flops 80000000000 | bytes 16000000 | tf_op jit(solution)/shard_map/mixer_backward/pallas_call | solution.py:471
  347.2 13.4 %project_back.1 = (bf16[2048,1024]{1,0:T(8,128)(2,1)}, bf16[1024,768]{1,0:T(8,128)(2,1)}, f32[8,1024]{1,0:T(8,128)}) custom-call(bf16[2048,1024]{1,0:T(8,128)(2,1)} %pad_maximum_fusion.inputs, f32[2,1024]{1,0:T(2,128)} %copy.311.norm, bf16[1024,768]{1,0:T(8,128)(2,1)} %all-gather.10.cloned.1.call-done.weight, bf16[2048,768]{1,0:T(8,128)(2,1)} %get-tuple-element.52.grad), custom_call_target="tpu_custom_call" | custom-call | flops 6442450944 | bytes 16000000 | tf_op jit(solution)/shard_map/project_back/pallas_call | solution.py:570
  368.1 19.0 %collective-permute-done.33 = bf16[2,16,32,512]{3,2,1,0:T(8,128)(2,1)} collective-permute-done((bf16[2,16,32,512]{3,2,1,0:T(8,128)(2,1)}, bf16[2,16,32,512]{3,2,1,0:T(8,128)(2,1)}, u32[]{:S(2)}, u32[]{:S(2)}) %collective-permute-start.33) | collective-permute-done | bytes 1048608 | tf_op jit(solution)/shard_map/ppermute | solution.py:770
  387.2 2.6 add_convert_fusion.1
  393.2 2.6 convolution_convert_fusion
  400.4 4.8 convolution_multiply_fusion.2
  405.3 2.9 multiply_reduce_fusion.4
  408.1 2.4 fusion.48
  410.6 3.3 fusion.17
  413.9 3.0 fusion.50
  418.0 35.3 %collective-permute-done.34 = bf16[2,16,32,512]{3,2,1,0:T(8,128)(2,1)} collective-permute-done((bf16[2,16,32,512]{3,2,1,0:T(8,128)(2,1)}, bf16[2,16,32,512]{3,2,1,0:T(8,128)(2,1)}, u32[]{:S(2)}, u32[]{:S(2)}) %collective-permute-start.34) | collective-permute-done | bytes 1048608 | tf_op jit(solution)/shard_map/ppermute | solution.py:770
  453.3 2.2 add_convert_fusion
  458.0 3.2 collective-permute-start.35
  476.9 3.5 collective-permute-start.36
  496.2 2.2 collective-permute-start.23
  503.7 5.2 collective-permute-start.24
  509.6 4.3 collective-permute-done.24
  514.0 9.0 %collective-permute-start.25 = (bf16[32,1024]{1,0:T(8,128)(2,1)S(1)}, bf16[32,1024]{1,0:T(8,128)(2,1)S(1)}, u32[]{:S(2)}, u32[]{:S(2)}) collective-permute-start(bf16[32,1024]{1,0:T(8,128)(2,1)S(1)} %get-tuple-element.279), channel_id=1, source_target_pairs={{0,8},{8,16},{16,24},{1,9},{9,17},{17,25},{2,10},{10,18},{18,26},{... | collective-permute-start | bytes 196616 | tf_op jit(solution)/shard_map/ppermute | solution.py:825
  525.0 4.2 collective-permute-done.28
  532.5 3.4 all-to-all-start.3
  537.2 2.4 reshape.507
  544.0 3.3 convert_reduce_fusion.1
  551.6 23.0 %small_sums.1 = (f32[32,128]{1,0:T(8,128)S(1)}, f32[32,8,128]{2,1,0:T(8,128)S(1)}) custom-call(f32[32,32,128]{2,1,0:T(8,128)S(1)} %pad_maximum_fusion.6.send), custom_call_target="tpu_custom_call" | custom-call | flops 1000000 | bytes 4000000 | tf_op jit(solution)/shard_map/small_sums/pallas_call | solution.py:912
  (374 shorter events, 133.6 us)
Async XLA Ops:
  7.2 94.7 %all-gather.12.cloned.1.call-start = ((), (), s32[]{:S(2)}) async-start(), calls=%async_computation.8 | async-start | bytes 1114112 | tf_op jit(solution)/shard_map/all_gather | solution.py:1050
  9.5 48.7 %collective-permute-start.2 = (bf16[1,512,512]{2,1,0:T(8,128)(2,1)S(1)}, bf16[1,512,512]{2,1,0:T(8,128)(2,1)S(1)}, u32[]{:S(2)}, u32[]{:S(2)}) collective-permute-start(bf16[1,512,512]{2,1,0:T(8,128)(2,1)S(1)} %get-tuple-element.274), channel_id=1, source_target_pairs={{0,2},{1,3},{2,0},{3,1},{4,6},{5,7},{6,4},{7,5},{8,10},{9,11},{10,... | collective-permute-start | bytes 1572872 | tf_op jit(solution)/shard_map/ppermute | solution.py:770
  12.5 57.6 %collective-permute-start = (bf16[1,512,512]{2,1,0:T(8,128)(2,1)S(1)}, bf16[1,512,512]{2,1,0:T(8,128)(2,1)}, u32[]{:S(2)}, u32[]{:S(2)}) collective-permute-start(bf16[1,512,512]{2,1,0:T(8,128)(2,1)S(1)} %get-tuple-element.273), channel_id=1, source_target_pairs={{0,1},{1,0},{2,3},{3,2},{4,5},{5,4},{6,7},{7,6},{8,9},{9,8},{10,11... | collective-permute-start | bytes 1572872 | tf_op jit(solution)/shard_map/ppermute | solution.py:770
  14.7 34.7 %all-to-all-start = ((bf16[32,3,4,256]{3,0,1,2:T(8,128)(2,1)}), bf16[32,3,4,256]{3,0,1,2:T(8,128)(2,1)S(1)}, u32[]{:S(2)}, u32[]{:S(2)}) async-start(bf16[32,3,4,256]{3,0,1,2:T(8,128)(2,1)} %bitcast.266), calls=%async_computation | async-start | bytes 393216 | tf_op jit(solution)/shard_map/all_to_all | solution.py:1026
  18.0 83.9 %all-gather.10.cloned.1.call-start = ((), (), s32[]{:S(2)}) async-start(), calls=%async_computation.6 | async-start | bytes 1769472 | tf_op jit(solution)/shard_map/all_gather | solution.py:1028
  20.3 59.0 %collective-permute-start.7 = (bf16[4,32,512]{2,1,0:T(8,128)(2,1)}, bf16[4,32,512]{2,1,0:T(8,128)(2,1)}, u32[]{:S(2)}, u32[]{:S(2)}) collective-permute-start(bf16[4,32,512]{2,1,0:T(8,128)(2,1)} %bitcast.268), channel_id=1, source_target_pairs={{0,4},{4,0},{1,5},{5,1},{2,6},{6,2},{3,7},{7,3},{8,12},{12,8},{9,1... | collective-permute-start | bytes 393224 | tf_op jit(solution)/shard_map/ppermute | solution.py:770
  50.2 98.5 %all-gather.14.cloned.1.call-start = ((), (), s32[]{:S(2)}) async-start(), calls=%async_computation.9 | async-start | bytes 2621440 | tf_op jit(solution)/shard_map/all_gather | solution.py:1043
  59.2 24.8 %collective-permute-start.3 = (bf16[2,512,512]{2,1,0:T(8,128)(2,1)}, bf16[2,512,512]{2,1,0:T(8,128)(2,1)}, u32[]{:S(2)}, u32[]{:S(2)}) collective-permute-start(bf16[2,512,512]{2,1,0:T(8,128)(2,1)} %pad_maximum_fusion.4), channel_id=1, source_target_pairs={{0,1},{1,0},{2,3},{3,2},{4,5},{5,4},{6,7},{7,6},{8,9},{9,8},{10,11... | collective-permute-start | bytes 3145736 | tf_op jit(solution)/shard_map/ppermute | solution.py:770
  72.2 23.4 %collective-permute-start.1 = (bf16[2,512,512]{2,1,0:T(8,128)(2,1)}, bf16[2,512,512]{2,1,0:T(8,128)(2,1)}, u32[]{:S(2)}, u32[]{:S(2)}) collective-permute-start(bf16[2,512,512]{2,1,0:T(8,128)(2,1)} %pad_maximum_fusion.3), channel_id=1, source_target_pairs={{0,2},{1,3},{2,0},{3,1},{4,6},{5,7},{6,4},{7,5},{8,10},{9,11},{10,... | collective-permute-start | bytes 3145736 | tf_op jit(solution)/shard_map/ppermute | solution.py:770
  101.9 43.5 %collective-permute-start.4 = (bf16[16,32,1024]{2,1,0:T(8,128)(2,1)}, bf16[16,32,1024]{2,1,0:T(8,128)(2,1)}, u32[]{:S(2)}, u32[]{:S(2)}) collective-permute-start(bf16[16,32,1024]{2,1,0:T(8,128)(2,1)} %bitcast.297), channel_id=1, source_target_pairs={{0,4},{4,0},{1,5},{5,1},{2,6},{6,2},{3,7},{7,3},{8,12},{12,8},{9,1... | collective-permute-start | bytes 3145736 | tf_op jit(solution)/shard_map/ppermute | solution.py:770
  139.6 17.9 %all-to-all-start.1 = ((bf16[4,512,256]{1,2,0:T(8,128)(2,1)}), bf16[4,512,256]{1,2,0:T(8,128)(2,1)S(1)}, u32[]{:S(2)}, u32[]{:S(2)}) async-start(bf16[4,512,256]{1,2,0:T(8,128)(2,1)} %copy.291), calls=%async_computation.1 | async-start | bytes 2097152 | tf_op jit(solution)/shard_map/all_to_all | solution.py:1079
  143.3 387.5 %reduce-scatter.5.cloned.1.call-start = ((), (), s32[]{:S(2)}) async-start(), calls=%async_computation.7 | async-start | bytes 1769472 | tf_op jit(solution)/shard_map/reduce_scatter | solution.py:1124
  143.7 20.1 %collective-permute-start.6 = (bf16[512,1024]{1,0:T(8,128)(2,1)}, bf16[512,1024]{1,0:T(8,128)(2,1)}, u32[]{:S(2)}, u32[]{:S(2)}) collective-permute-start(bf16[512,1024]{1,0:T(8,128)(2,1)} %bitcast.41.grad_own), channel_id=1, source_target_pairs={{0,4},{4,0},{1,5},{5,1},{2,6},{6,2},{3,7},{7,3},{8,12},{12,8},{9,1... | collective-permute-start | bytes 3145736 | tf_op jit(solution)/shard_map/ppermute | solution.py:770
  151.8 28.3 %collective-permute-start.8 = (bf16[2,16,32,512]{3,2,1,0:T(8,128)(2,1)}, bf16[2,16,32,512]{3,2,1,0:T(8,128)(2,1)}, u32[]{:S(2)}, u32[]{:S(2)}) collective-permute-start(bf16[2,16,32,512]{3,2,1,0:T(8,128)(2,1)} %bitcast.49.rest_0_), channel_id=1, source_target_pairs={{0,1},{1,0},{2,3},{3,2},{4,5},{5,4},{6,7},{7,6},{8,9},{9,8},{10,11... | collective-permute-start | bytes 3145736 | tf_op jit(solution)/shard_map/ppermute | solution.py:770
  153.8 50.4 %collective-permute-start.10 = (bf16[2,16,32,512]{3,2,1,0:T(8,128)(2,1)}, bf16[2,16,32,512]{3,2,1,0:T(8,128)(2,1)}, u32[]{:S(2)}, u32[]{:S(2)}) collective-permute-start(bf16[2,16,32,512]{3,2,1,0:T(8,128)(2,1)} %bitcast.49.rest_0_), channel_id=1, source_target_pairs={{0,2},{1,3},{2,0},{3,1},{4,6},{5,7},{6,4},{7,5},{8,10},{9,11},{10,... | collective-permute-start | bytes 3145736 | tf_op jit(solution)/shard_map/ppermute | solution.py:770
  155.3 47.3 %collective-permute-start.11 = (bf16[2,16,32,512]{3,2,1,0:T(8,128)(2,1)}, bf16[2,16,32,512]{3,2,1,0:T(8,128)(2,1)}, u32[]{:S(2)}, u32[]{:S(2)}) collective-permute-start(bf16[2,16,32,512]{3,2,1,0:T(8,128)(2,1)} %bitcast.50.rest_1_), channel_id=1, source_target_pairs={{0,2},{1,3},{2,0},{3,1},{4,6},{5,7},{6,4},{7,5},{8,10},{9,11},{10,... | collective-permute-start | bytes 3145736 | tf_op jit(solution)/shard_map/ppermute | solution.py:770
  155.8 48.4 %collective-permute-start.9 = (bf16[2,16,32,512]{3,2,1,0:T(8,128)(2,1)}, bf16[2,16,32,512]{3,2,1,0:T(8,128)(2,1)}, u32[]{:S(2)}, u32[]{:S(2)}) collective-permute-start(bf16[2,16,32,512]{3,2,1,0:T(8,128)(2,1)} %bitcast.50.rest_1_), channel_id=1, source_target_pairs={{0,1},{1,0},{2,3},{3,2},{4,5},{5,4},{6,7},{7,6},{8,9},{9,8},{10,11... | collective-permute-start | bytes 3145736 | tf_op jit(solution)/shard_map/ppermute | solution.py:770
  163.8 40.4 %collective-permute-start.5 = (bf16[512,1024]{1,0:T(8,128)(2,1)}, bf16[512,1024]{1,0:T(8,128)(2,1)}, u32[]{:S(2)}, u32[]{:S(2)}) collective-permute-start(bf16[512,1024]{1,0:T(8,128)(2,1)} %add_convert_fusion.7.normed_own), channel_id=1, source_target_pairs={{0,4},{4,0},{1,5},{5,1},{2,6},{6,2},{3,7},{7,3},{8,12},{12,8},{9,1... | collective-permute-start | bytes 3145736 | tf_op jit(solution)/shard_map/ppermute | solution.py:770
  180.1 44.2 %collective-permute-start.12 = (bf16[2,16,32,512]{3,2,1,0:T(8,128)(2,1)}, bf16[2,16,32,512]{3,2,1,0:T(8,128)(2,1)}, u32[]{:S(2)}, u32[]{:S(2)}) collective-permute-start(bf16[2,16,32,512]{3,2,1,0:T(8,128)(2,1)} %collective-permute-done.8.rest_2_), channel_id=1, source_target_pairs={{0,2},{1,3},{2,0},{3,1},{4,6},{5,7},{6,4},{7,5},{8,10},{9,11},{10,... | collective-permute-start | bytes 3145736 | tf_op jit(solution)/shard_map/ppermute | solution.py:770
  202.6 24.1 %collective-permute-start.13 = (bf16[2,16,32,512]{3,2,1,0:T(8,128)(2,1)}, bf16[2,16,32,512]{3,2,1,0:T(8,128)(2,1)}, u32[]{:S(2)}, u32[]{:S(2)}) collective-permute-start(bf16[2,16,32,512]{3,2,1,0:T(8,128)(2,1)} %collective-permute-done.11.rest_5_), channel_id=1, source_target_pairs={{0,1},{1,0},{2,3},{3,2},{4,5},{5,4},{6,7},{7,6},{8,9},{9,8},{10,11... | collective-permute-start | bytes 3145736 | tf_op jit(solution)/shard_map/ppermute | solution.py:770
  267.2 5.9 collective-permute-start.14
  360.6 181.2 %reduce-scatter.7.cloned.1.call-start = ((), (), s32[]{:S(2)}) async-start(), calls=%async_computation.10 | async-start | bytes 5242880
  360.7 26.5 %collective-permute-start.33 = (bf16[2,16,32,512]{3,2,1,0:T(8,128)(2,1)}, bf16[2,16,32,512]{3,2,1,0:T(8,128)(2,1)}, u32[]{:S(2)}, u32[]{:S(2)}) collective-permute-start(bf16[2,16,32,512]{3,2,1,0:T(8,128)(2,1)} %get-tuple-element.67), channel_id=1, source_target_pairs={{0,2},{1,3},{2,0},{3,1},{4,6},{5,7},{6,4},{7,5},{8,10},{9,11},{10,... | collective-permute-start | bytes 3145736 | tf_op jit(solution)/shard_map/ppermute | solution.py:770
  362.7 27.9 %collective-permute-start.30 = (bf16[2,16,32,512]{3,2,1,0:T(8,128)(2,1)}, bf16[2,16,32,512]{3,2,1,0:T(8,128)(2,1)}, u32[]{:S(2)}, u32[]{:S(2)}) collective-permute-start(bf16[2,16,32,512]{3,2,1,0:T(8,128)(2,1)} %get-tuple-element.63), channel_id=1, source_target_pairs={{0,1},{1,0},{2,3},{3,2},{4,5},{5,4},{6,7},{7,6},{8,9},{9,8},{10,11... | collective-permute-start | bytes 3145736 | tf_op jit(solution)/shard_map/ppermute | solution.py:770
  364.7 53.3 %collective-permute-start.32 = (bf16[2,16,32,512]{3,2,1,0:T(8,128)(2,1)}, bf16[2,16,32,512]{3,2,1,0:T(8,128)(2,1)}, u32[]{:S(2)}, u32[]{:S(2)}) collective-permute-start(bf16[2,16,32,512]{3,2,1,0:T(8,128)(2,1)} %get-tuple-element.65), channel_id=1, source_target_pairs={{0,2},{1,3},{2,0},{3,1},{4,6},{5,7},{6,4},{7,5},{8,10},{9,11},{10,... | collective-permute-start | bytes 3145736 | tf_op jit(solution)/shard_map/ppermute | solution.py:770
  365.6 89.9 %collective-permute-start.29 = (bf16[2,16,32,512]{3,2,1,0:T(8,128)(2,1)}, bf16[2,16,32,512]{3,2,1,0:T(8,128)(2,1)}, u32[]{:S(2)}, u32[]{:S(2)}) collective-permute-start(bf16[2,16,32,512]{3,2,1,0:T(8,128)(2,1)} %get-tuple-element.61), channel_id=1, source_target_pairs={{0,1},{1,0},{2,3},{3,2},{4,5},{5,4},{6,7},{7,6},{8,9},{9,8},{10,11... | collective-permute-start | bytes 3145736 | tf_op jit(solution)/shard_map/ppermute | solution.py:770
  389.7 63.6 %collective-permute-start.34 = (bf16[2,16,32,512]{3,2,1,0:T(8,128)(2,1)}, bf16[2,16,32,512]{3,2,1,0:T(8,128)(2,1)}, u32[]{:S(2)}, u32[]{:S(2)}) collective-permute-start(bf16[2,16,32,512]{3,2,1,0:T(8,128)(2,1)} %add_convert_fusion.1), channel_id=1, source_target_pairs={{0,1},{1,0},{2,3},{3,2},{4,5},{5,4},{6,7},{7,6},{8,9},{9,8},{10,11... | collective-permute-start | bytes 3145736 | tf_op jit(solution)/shard_map/ppermute | solution.py:770
  392.3 63.2 %collective-permute-start.31 = (bf16[2,16,32,512]{3,2,1,0:T(8,128)(2,1)S(1)}, bf16[2,16,32,512]{3,2,1,0:T(8,128)(2,1)}, u32[]{:S(2)}, u32[]{:S(2)}) collective-permute-start(bf16[2,16,32,512]{3,2,1,0:T(8,128)(2,1)S(1)} %add_convert_fusion.4), channel_id=1, source_target_pairs={{0,2},{1,3},{2,0},{3,1},{4,6},{5,7},{6,4},{7,5},{8,10},{9,11},{10,... | collective-permute-start | bytes 3145736 | tf_op jit(solution)/shard_map/ppermute | solution.py:770
  398.1 64.1 %collective-permute-start.16 = (bf16[4,4,32,1024]{3,2,0,1:T(8,128)(2,1)}, bf16[4,4,32,1024]{3,2,0,1:T(8,128)(2,1)}, u32[]{:S(2)}, u32[]{:S(2)}) collective-permute-start(bf16[4,4,32,1024]{3,2,0,1:T(8,128)(2,1)} %bitcast.265), channel_id=1, source_target_pairs={{0,4},{4,0},{1,5},{5,1},{2,6},{6,2},{3,7},{7,3},{8,12},{12,8},{9,1... | collective-permute-start | bytes 3145736 | tf_op jit(solution)/shard_map/ppermute | solution.py:770
  458.0 15.8 %collective-permute-start.35 = (bf16[16,32,512]{2,1,0:T(8,128)(2,1)S(1)}, bf16[16,32,512]{2,1,0:T(8,128)(2,1)S(1)}, u32[]{:S(2)}, u32[]{:S(2)}) collective-permute-start(bf16[16,32,512]{2,1,0:T(8,128)(2,1)S(1)} %get-tuple-element.260), channel_id=1, source_target_pairs={{0,8},{1,9},{2,10},{3,11},{4,12},{5,13},{6,14},{7,15}} | collective-permute-start | bytes 1572872 | tf_op jit(solution)/shard_map/ppermute | solution.py:825
  461.3 13.9 %collective-permute-start.38 = (bf16[16,32,512]{2,1,0:T(8,128)(2,1)S(1)}, bf16[16,32,512]{2,1,0:T(8,128)(2,1)S(1)}, u32[]{:S(2)}, u32[]{:S(2)}) collective-permute-start(bf16[16,32,512]{2,1,0:T(8,128)(2,1)S(1)} %get-tuple-element.261), channel_id=1, source_target_pairs={{24,16},{25,17},{26,18},{27,19},{28,20},{29,21},{30,22},{31,23}} | collective-permute-start | bytes 1572872 | tf_op jit(solution)/shard_map/ppermute | solution.py:828
  464.0 6.4 %collective-permute-start.18 = (bf16[2,32,1024]{2,1,0:T(8,128)(2,1)S(1)}, bf16[2,32,1024]{2,1,0:T(8,128)(2,1)S(1)}, u32[]{:S(2)}, u32[]{:S(2)}) collective-permute-start(bf16[2,32,1024]{2,1,0:T(8,128)(2,1)S(1)} %get-tuple-element.288), channel_id=1, source_target_pairs={{0,1},{1,0},{2,3},{3,2},{4,5},{5,4},{6,7},{7,6},{8,9},{9,8},{10,11... | collective-permute-start | bytes 393224 | tf_op jit(solution)/shard_map/ppermute | solution.py:770
  465.5 7.1 %collective-permute-start.21 = (bf16[2,32,1024]{2,1,0:T(8,128)(2,1)S(1)}, bf16[2,32,1024]{2,1,0:T(8,128)(2,1)S(1)}, u32[]{:S(2)}, u32[]{:S(2)}) collective-permute-start(bf16[2,32,1024]{2,1,0:T(8,128)(2,1)S(1)} %get-tuple-element.287), channel_id=1, source_target_pairs={{0,2},{1,3},{2,0},{3,1},{4,6},{5,7},{6,4},{7,5},{8,10},{9,11},{10,... | collective-permute-start | bytes 393224 | tf_op jit(solution)/shard_map/ppermute | solution.py:770
  465.8 14.6 %collective-permute-start.17 = (bf16[2,32,1024]{2,1,0:T(8,128)(2,1)S(1)}, bf16[2,32,1024]{2,1,0:T(8,128)(2,1)S(1)}, u32[]{:S(2)}, u32[]{:S(2)}) collective-permute-start(bf16[2,32,1024]{2,1,0:T(8,128)(2,1)S(1)} %slice_bitcast_fusion.9), channel_id=1, source_target_pairs={{0,1},{1,0},{2,3},{3,2},{4,5},{5,4},{6,7},{7,6},{8,9},{9,8},{10,11... | collective-permute-start | bytes 393224 | tf_op jit(solution)/shard_map/ppermute | solution.py:770
  470.4 24.5 %collective-permute-start.20 = (bf16[2,32,1024]{2,1,0:T(8,128)(2,1)}, bf16[2,32,1024]{2,1,0:T(8,128)(2,1)}, u32[]{:S(2)}, u32[]{:S(2)}) collective-permute-start(bf16[2,32,1024]{2,1,0:T(8,128)(2,1)} %slice_bitcast_fusion.5), channel_id=1, source_target_pairs={{0,2},{1,3},{2,0},{3,1},{4,6},{5,7},{6,4},{7,5},{8,10},{9,11},{10,... | collective-permute-start | bytes 393224 | tf_op jit(solution)/shard_map/ppermute | solution.py:770
  472.6 22.4 %collective-permute-start.19 = (bf16[2,32,1024]{2,1,0:T(8,128)(2,1)}, bf16[2,32,1024]{2,1,0:T(8,128)(2,1)}, u32[]{:S(2)}, u32[]{:S(2)}) collective-permute-start(bf16[2,32,1024]{2,1,0:T(8,128)(2,1)} %fusion.59), channel_id=1, source_target_pairs={{0,2},{1,3},{2,0},{3,1},{4,6},{5,7},{6,4},{7,5},{8,10},{9,11},{10,... | collective-permute-start | bytes 393224 | tf_op jit(solution)/shard_map/ppermute | solution.py:770
  473.8 21.1 %collective-permute-start.22 = (bf16[2,32,1024]{2,1,0:T(8,128)(2,1)}, bf16[2,32,1024]{2,1,0:T(8,128)(2,1)}, u32[]{:S(2)}, u32[]{:S(2)}) collective-permute-start(bf16[2,32,1024]{2,1,0:T(8,128)(2,1)} %fusion.57), channel_id=1, source_target_pairs={{0,1},{1,0},{2,3},{3,2},{4,5},{5,4},{6,7},{7,6},{8,9},{9,8},{10,11... | collective-permute-start | bytes 393224 | tf_op jit(solution)/shard_map/ppermute | solution.py:770
  476.9 22.2 %collective-permute-start.36 = (bf16[16,32,512]{2,1,0:T(8,128)(2,1)}, bf16[16,32,512]{2,1,0:T(8,128)(2,1)}, u32[]{:S(2)}, u32[]{:S(2)}) collective-permute-start(bf16[16,32,512]{2,1,0:T(8,128)(2,1)} %get-tuple-element.258), channel_id=1, source_target_pairs={{0,8},{8,16},{1,9},{9,17},{2,10},{10,18},{3,11},{11,19},{4,12},{12... | collective-permute-start | bytes 1572872 | tf_op jit(solution)/shard_map/ppermute | solution.py:825
  480.4 18.7 %collective-permute-start.39 = (bf16[16,32,512]{2,1,0:T(8,128)(2,1)}, bf16[16,32,512]{2,1,0:T(8,128)(2,1)}, u32[]{:S(2)}, u32[]{:S(2)}) collective-permute-start(bf16[16,32,512]{2,1,0:T(8,128)(2,1)} %get-tuple-element.259), channel_id=1, source_target_pairs={{24,16},{16,8},{25,17},{17,9},{26,18},{18,10},{27,19},{19,11},{28,... | collective-permute-start | bytes 1572872 | tf_op jit(solution)/shard_map/ppermute | solution.py:828
  496.2 7.4 %collective-permute-start.23 = (bf16[32,1024]{1,0:T(8,128)(2,1)S(1)}, bf16[32,1024]{1,0:T(8,128)(2,1)S(1)}, u32[]{:S(2)}, u32[]{:S(2)}) collective-permute-start(bf16[32,1024]{1,0:T(8,128)(2,1)S(1)} %get-tuple-element.283), channel_id=1, source_target_pairs={{0,8},{1,9},{2,10},{3,11},{4,12},{5,13},{6,14},{7,15}} | collective-permute-start | bytes 196616 | tf_op jit(solution)/shard_map/ppermute | solution.py:825
  498.4 5.2 collective-permute-start.26
  501.0 23.4 %collective-permute-start.37 = (bf16[16,32,512]{2,1,0:T(8,128)(2,1)S(1)}, bf16[16,32,512]{2,1,0:T(8,128)(2,1)S(1)}, u32[]{:S(2)}, u32[]{:S(2)}) collective-permute-start(bf16[16,32,512]{2,1,0:T(8,128)(2,1)S(1)} %get-tuple-element.256), channel_id=1, source_target_pairs={{0,8},{8,16},{16,24},{1,9},{9,17},{17,25},{2,10},{10,18},{18,26},{... | collective-permute-start | bytes 1572872 | tf_op jit(solution)/shard_map/ppermute | solution.py:825
  502.3 22.1 %collective-permute-start.40 = (bf16[16,32,512]{2,1,0:T(8,128)(2,1)S(1)}, bf16[16,32,512]{2,1,0:T(8,128)(2,1)S(1)}, u32[]{:S(2)}, u32[]{:S(2)}) collective-permute-start(bf16[16,32,512]{2,1,0:T(8,128)(2,1)S(1)} %get-tuple-element.257), channel_id=1, source_target_pairs={{24,16},{16,8},{8,0},{25,17},{17,9},{9,1},{26,18},{18,10},{10,2},{... | collective-permute-start | bytes 1572872 | tf_op jit(solution)/shard_map/ppermute | solution.py:828
  503.7 10.2 %collective-permute-start.24 = (bf16[32,1024]{1,0:T(8,128)(2,1)S(1)}, bf16[32,1024]{1,0:T(8,128)(2,1)S(1)}, u32[]{:S(2)}, u32[]{:S(2)}) collective-permute-start(bf16[32,1024]{1,0:T(8,128)(2,1)S(1)} %get-tuple-element.281), channel_id=1, source_target_pairs={{0,8},{8,16},{1,9},{9,17},{2,10},{10,18},{3,11},{11,19},{4,12},{12... | collective-permute-start | bytes 196616 | tf_op jit(solution)/shard_map/ppermute | solution.py:825
  514.0 10.9 %collective-permute-start.25 = (bf16[32,1024]{1,0:T(8,128)(2,1)S(1)}, bf16[32,1024]{1,0:T(8,128)(2,1)S(1)}, u32[]{:S(2)}, u32[]{:S(2)}) collective-permute-start(bf16[32,1024]{1,0:T(8,128)(2,1)S(1)} %get-tuple-element.279), channel_id=1, source_target_pairs={{0,8},{8,16},{16,24},{1,9},{9,17},{17,25},{2,10},{10,18},{18,26},{... | collective-permute-start | bytes 196616 | tf_op jit(solution)/shard_map/ppermute | solution.py:825
  523.0 6.2 %collective-permute-start.28 = (bf16[32,1024]{1,0:T(8,128)(2,1)S(1)}, bf16[32,1024]{1,0:T(8,128)(2,1)S(1)}, u32[]{:S(2)}, u32[]{:S(2)}) collective-permute-start(bf16[32,1024]{1,0:T(8,128)(2,1)S(1)} %get-tuple-element.280), channel_id=1, source_target_pairs={{24,16},{16,8},{8,0},{25,17},{17,9},{9,1},{26,18},{18,10},{10,2},{... | collective-permute-start | bytes 196616 | tf_op jit(solution)/shard_map/ppermute | solution.py:828
  524.9 11.0 %collective-permute-start.41 = (bf16[4,32,512]{2,1,0:T(8,128)(2,1)S(1)}, bf16[4,32,512]{2,1,0:T(8,128)(2,1)S(1)}, u32[]{:S(2)}, u32[]{:S(2)}) collective-permute-start(bf16[4,32,512]{2,1,0:T(8,128)(2,1)S(1)} %fusion.68), channel_id=1, source_target_pairs={{0,4},{4,0},{1,5},{5,1},{2,6},{6,2},{3,7},{7,3},{8,12},{12,8},{9,1... | collective-permute-start | bytes 393224 | tf_op jit(solution)/shard_map/ppermute | solution.py:770
  532.5 8.5 %all-to-all-start.3 = ((bf16[4,32,3,256]{3,1,2,0:T(8,128)(2,1)}), bf16[4,32,3,256]{3,1,2,0:T(8,128)(2,1)S(1)}, u32[]{:S(2)}, u32[]{:S(2)}) async-start(bf16[4,32,3,256]{3,1,2,0:T(8,128)(2,1)} %copy.304), calls=%async_computation.4 | async-start | bytes 393216 | tf_op jit(solution)/shard_map/all_to_all | solution.py:1179
  (64 other events, 738.3 us)
Sparse Core Ops, SparseCore 0:
  10.8 59.2 all-gather.11
  71.7 24.7 all-gather.9
  98.7 45.4 all-gather.13
  360.8 30.8 reduce-scatter.4
  394.5 73.4 reduce-scatter.6
